TPU v7x, 256 devices: a whole 4x4x8 slice. The times are simulated.
256 devices in a mesh: dp: 8 (over y, core), tm: 32 (over x, z).
Axes of the slice: x: 4, y: 4, z: 8, core: 2. Of those that a mesh axis runs over, the one named last changes fastest.
Arguments:
- waveform: bfloat16 [8, 4096, 256], P('dp', 'tm'), may hold values from -6 to 6
- speaker_ids: int32 [8], P('dp'), may hold values from 0 to 6111
- speaker_table: bfloat16 [6112, 256], replicated, may hold values from 0.099609375 to 1.8984375
- stencil_taps: float32 [3, 256], replicated, may hold values from -3.5 to 3.5
- skip_gain: float32 [256], replicated, may hold values from 0.5 to 1.5
- filters: float32 [4096, 256], P('tm'), may hold values from -0.09375 to 0.09375
- cotangent: bfloat16 [8, 4096, 256], P('dp', 'tm'), may hold values from -6 to 6
Outputs:
- layer_out: float32 [8, 4096, 256], P('dp', 'tm')
- grad_waveform: float32 [8, 4096, 256], P('dp', 'tm')
- filter_grad: float32 [4096, 256], P('tm')
All inputs are finite; a program needn't handle non-finite values.
Results may differ from a plain program's by a relative error of at most 0.0003.
Values may be sent and summed in bfloat16 or wider, within the bound.
A program may use at most 64 MiB of HBM per device.

v0:
```python
import math

import jax
import jax.numpy as jnp
from jax import lax
from jax.sharding import PartitionSpec as P

PRECISE = lax.Precision.HIGHEST


def from_partner(block, axis, bit):
    count = lax.axis_size(axis)
    route = []
    for low in range(count):
        high = low | 1 << bit
        if high != low and high < count:
            route += [(low, high), (high, low)]
    return lax.ppermute(block, axis, route)


def with_halo(block, sides, width):
    for axis, dim in sides:
        count = lax.axis_size(axis)
        forward = [(i, i + 1) for i in range(count - 1)]
        backward = [(target, source) for source, target in forward]
        low = lax.ppermute(
            lax.slice_in_dim(block, block.shape[dim] - width, None, axis=dim), axis, forward
        )
        high = lax.ppermute(lax.slice_in_dim(block, 0, width, axis=dim), axis, backward)
        block = jnp.concatenate([low, block, high], axis=dim)
    return block


def stencil_apply(padded, stencil_taps):
    return (
        stencil_taps[0] * padded[:, :-2]
        + stencil_taps[1] * padded[:, 1:-1]
        + stencil_taps[2] * padded[:, 2:]
    )


def dense_tables(order_size, direction):
    indices = jnp.arange(order_size, dtype=jnp.int32)
    product = indices[:, None] * indices[None, :] % order_size
    phase_angle = 2.0 * math.pi / order_size * product.astype(jnp.float32)
    return (jnp.cos(phase_angle), direction * jnp.sin(phase_angle))


def split_length(local_len):
    best_factor = 1
    for factor in range(1, math.isqrt(local_len) + 1):
        if local_len % factor == 0:
            best_factor = factor
    return (best_factor, local_len // best_factor)


def outer_mix(matrix_table, field_data):
    return jnp.einsum("ka,bamc->bkmc", matrix_table, field_data, precision=PRECISE)


def inner_mix(matrix_table, field_data):
    return jnp.einsum("qm,bkmc->bqkc", matrix_table, field_data, precision=PRECISE)


def across_devices(shaped, cos_table, sin_table):
    real_part = shaped[0]
    imag_part = shaped[1]
    out_real = outer_mix(cos_table, real_part) - outer_mix(sin_table, imag_part)
    out_imag = outer_mix(cos_table, imag_part) + outer_mix(sin_table, real_part)
    return jnp.stack([out_real, out_imag])


def complex_scale(stacked, cos_value, sin_value):
    real_part = stacked[0]
    imag_part = stacked[1]
    return jnp.stack(
        [
            real_part * cos_value - imag_part * sin_value,
            real_part * sin_value + imag_part * cos_value,
        ]
    )


def complex_dft(stacked, direction):
    local_len = stacked.shape[2]
    outer_len, inner_len = split_length(local_len)
    shaped = stacked.reshape(2, stacked.shape[1], outer_len, inner_len, stacked.shape[3])
    outer_cos, outer_sin = dense_tables(outer_len, direction)
    shaped = across_devices(shaped, outer_cos, outer_sin)
    outer_idx = jnp.arange(outer_len, dtype=jnp.int32)[:, None]
    inner_idx = jnp.arange(inner_len, dtype=jnp.int32)[None, :]
    grid_angle = (
        direction
        * 2.0
        * math.pi
        / local_len
        * (outer_idx * inner_idx % local_len).astype(jnp.float32)
    )
    shaped = complex_scale(shaped, jnp.cos(grid_angle)[:, :, None], jnp.sin(grid_angle)[:, :, None])
    inner_cos, inner_sin = dense_tables(inner_len, direction)
    real_part = shaped[0]
    imag_part = shaped[1]
    out_real = inner_mix(inner_cos, real_part) - inner_mix(inner_sin, imag_part)
    out_imag = inner_mix(inner_cos, imag_part) + inner_mix(inner_sin, real_part)
    result = jnp.stack([out_real, out_imag])
    return result.reshape(2, stacked.shape[1], local_len, stacked.shape[3])


def complex_product(first_value, second_value):
    return jnp.stack(
        [
            first_value[0] * second_value[0] - first_value[1] * second_value[1],
            first_value[0] * second_value[1] + first_value[1] * second_value[0],
        ]
    )


def conjugate(stacked):
    return jnp.stack([stacked[0], -stacked[1]])


def reverse_bits(position, sections):
    result = jnp.zeros((), jnp.int32)
    for section_bit in range(sections):
        result = result + (position >> section_bit & 1) * (1 << sections - 1 - section_bit)
    return result


def cross_twiddle(frequency, local_len, total_len, direction):
    samples = jnp.arange(local_len, dtype=jnp.int32)
    phase_angle = (
        direction
        * 2.0
        * math.pi
        / total_len
        * (frequency * samples % total_len).astype(jnp.float32)
    )
    return (jnp.cos(phase_angle)[None, :, None], jnp.sin(phase_angle)[None, :, None])


def forward_transform(field_data):
    group_size = lax.axis_size("tm")
    position = lax.axis_index("tm")
    sections = group_size.bit_length() - 1
    local_len = field_data.shape[1]
    stacked = jnp.stack([field_data, jnp.zeros_like(field_data)])
    remaining = list(reversed(range(sections)))
    for section_bit in remaining:
        half_span = 1 << section_bit
        partner = from_partner(stacked, "tm", section_bit)
        upper_bit = position >> section_bit & 1
        phase_angle = -2.0 * math.pi / (2 * half_span) * (position % half_span).astype(jnp.float32)
        lower_value = stacked + partner
        upper_value = complex_scale(partner - stacked, jnp.cos(phase_angle), jnp.sin(phase_angle))
        stacked = jnp.where(upper_bit == 1, upper_value, lower_value)
    frequency = reverse_bits(position, sections)
    cos_value, sin_value = cross_twiddle(frequency, local_len, local_len * group_size, -1.0)
    stacked = complex_scale(stacked, cos_value, sin_value)
    return complex_dft(stacked, -1.0)


def inverse_transform(stacked):
    group_size = lax.axis_size("tm")
    position = lax.axis_index("tm")
    sections = group_size.bit_length() - 1
    local_len = stacked.shape[2]
    total_len = local_len * group_size
    frequency = reverse_bits(position, sections)
    stacked = complex_dft(stacked, 1.0)
    cos_value, sin_value = cross_twiddle(frequency, local_len, total_len, 1.0)
    stacked = complex_scale(stacked, cos_value, sin_value)
    for section_bit in range(sections):
        half_span = 1 << section_bit
        partner = from_partner(stacked, "tm", section_bit)
        upper_bit = position >> section_bit & 1
        phase_angle = 2.0 * math.pi / (2 * half_span) * (position % half_span).astype(jnp.float32)
        cos_turn = jnp.cos(phase_angle)
        sin_turn = jnp.sin(phase_angle)
        lower_value = stacked + complex_scale(partner, cos_turn, sin_turn)
        upper_value = partner - complex_scale(stacked, cos_turn, sin_turn)
        stacked = jnp.where(upper_bit == 1, upper_value, lower_value)
    return stacked / total_len


def local(waveform, speaker_ids, speaker_table, stencil_taps, skip_gain, filters, cotangent):
    speakers = speaker_table.shape[0]
    speaker_match = (speaker_ids[:, None] == jnp.arange(speakers, dtype=jnp.int32)[None, :]).astype(
        jnp.bfloat16
    )
    speaker_rows = jnp.dot(speaker_match, speaker_table, preferred_element_type=jnp.float32)
    padded = with_halo(waveform, (("tm", 1),), 1)
    value_field = stencil_apply(padded.astype(jnp.float32), stencil_taps) * speaker_rows[:, None, :]
    value_spectrum = forward_transform(value_field)
    filter_spectrum = forward_transform(filters[None])
    convolved = inverse_transform(complex_product(value_spectrum, filter_spectrum))[0]
    layer_out = convolved + skip_gain * value_field
    grad_field = cotangent.astype(jnp.float32)
    grad_spectrum = forward_transform(grad_field)
    grad_value_spectrum = complex_product(grad_spectrum, conjugate(filter_spectrum))
    filter_term = jnp.sum(
        complex_product(conjugate(value_spectrum), grad_spectrum), axis=1, keepdims=True
    )
    packed = jnp.stack(
        [grad_value_spectrum[0] - filter_term[1], grad_value_spectrum[1] + filter_term[0]]
    )
    restored = inverse_transform(packed)
    grad_value = restored[0] + skip_gain * grad_field
    filter_grad = lax.psum(restored[1][0], "dp")
    grad_mid = grad_value * speaker_rows[:, None, :]
    grad_padded = with_halo(grad_mid, (("tm", 1),), 1)
    grad_waveform = stencil_apply(grad_padded, stencil_taps[::-1])
    return (layer_out, grad_waveform, filter_grad)


def solution(mesh):
    return jax.shard_map(
        local,
        mesh=mesh,
        in_specs=(P("dp", "tm", None), P("dp"), P(), P(), P(), P("tm", None), P("dp", "tm", None)),
        out_specs=(P("dp", "tm", None), P("dp", "tm", None), P("tm", None)),
        check_vma=False,
    )
```

profile of v0, /device:TPU:1, one launch (start us, length us, event | category | flops | bytes accessed | tf_op | source)
XLA Modules:
  0.0 309.2 jit_solution(7818577165591072163)
XLA Ops:
  7.2 1.0 convert_bitcast_fusion
  8.2 0.7 stack.124
  8.9 3.6 %collective-permute-start.17 = (f32[2,1,128,256]{3,2,1,0:T(8,128)}, f32[2,1,128,256]{3,2,1,0:T(8,128)}, u32[]{:S(2)}, u32[]{:S(2)}) collective-permute-start(f32[2,1,128,256]{3,2,1,0:T(8,128)} %stack.124), channel_id=1, source_target_pairs={{0,16},{16,0},{1,17},{17,1},{2,18},{18,2},{3,19},{19,3},{4,20},{20... | collective-permute-start | bytes 786440 | tf_op jit(solution)/shard_map/ppermute | solution.py:18
  12.5 1.6 stack.103
  14.1 1.3 fusion.420
  15.4 1.3 collective-permute-start.1
  16.7 5.0 %collective-permute-start = (bf16[1,1,256]{2,1,0:T(2,128)(2,1)}, bf16[1,1,256]{2,1,0:T(2,128)(2,1)}, u32[]{:S(2)}, u32[]{:S(2)}) collective-permute-start(bf16[1,1,256]{2,1,0:T(2,128)(2,1)} %get-tuple-element.101), channel_id=1, source_target_pairs={{0,1},{1,2},{2,3},{3,4},{4,5},{5,6},{6,7},{7,8},{8,9},{9,10},{10,1... | collective-permute-start | bytes 1544 | tf_op jit(solution)/shard_map/ppermute | solution.py:26
  22.3 0.6 fusion.238
  23.0 0.7 multiply_sine_fusion.1
  24.6 0.6 reshape.2327
  25.2 1.4 fusion.421
  26.6 1.8 fusion.428
  29.0 0.9 maximum_convert_fusion
  29.9 0.7 fusion.432
  30.6 6.2 %collective-permute-start.2 = (f32[2,1,128,256]{3,2,1,0:T(8,128)S(1)}, f32[2,1,128,256]{3,2,1,0:T(8,128)S(1)}, u32[]{:S(2)}, u32[]{:S(2)}) collective-permute-start(f32[2,1,128,256]{3,2,1,0:T(8,128)S(1)} %stack.97), channel_id=1, source_target_pairs={{0,16},{16,0},{1,17},{17,1},{2,18},{18,2},{3,19},{19,3},{4,20},{20... | collective-permute-start | bytes 786440 | tf_op jit(solution)/shard_map/ppermute | solution.py:18
  36.8 1.0 pad_subtract_fusion
  37.8 0.9 pad_subtract_fusion.1
  38.8 1.0 maximum_select_fusion.10
  39.8 0.7 collective-permute-start.18
  40.5 0.9 collective-permute-start.8
  42.0 1.2 collective-permute-start.3
  43.3 5.0 %collective-permute-done.18 = f32[2,1,128,256]{3,2,1,0:T(8,128)S(1)} collective-permute-done((f32[2,1,128,256]{3,2,1,0:T(8,128)S(1)}, f32[2,1,128,256]{3,2,1,0:T(8,128)S(1)}, u32[]{:S(2)}, u32[]{:S(2)}) %collective-permute-start.18) | collective-permute-done | bytes 262176 | tf_op jit(solution)/shard_map/ppermute | solution.py:18
  48.3 1.0 fusion.434
  49.3 1.0 maximum_select_fusion.11
  50.4 2.9 collective-permute-start.19
  53.3 0.6 collective-permute-done.8
  54.1 2.9 collective-permute-start.9
  57.0 2.5 collective-permute-done.3
  59.7 2.9 collective-permute-start.4
  62.6 1.2 collective-permute-done.19
  64.1 14.2 %collective-permute-done.9 = f32[2,1,128,256]{3,2,1,0:T(8,128)S(1)} collective-permute-done((f32[2,1,128,256]{3,2,1,0:T(8,128)S(1)}, f32[2,1,128,256]{3,2,1,0:T(8,128)S(1)}, u32[]{:S(2)}, u32[]{:S(2)}) %collective-permute-start.9) | collective-permute-done | bytes 262176 | tf_op jit(solution)/shard_map/ppermute | solution.py:18
  78.5 10.6 %collective-permute-done.4 = f32[2,1,128,256]{3,2,1,0:T(8,128)S(1)} collective-permute-done((f32[2,1,128,256]{3,2,1,0:T(8,128)S(1)}, f32[2,1,128,256]{3,2,1,0:T(8,128)S(1)}, u32[]{:S(2)}, u32[]{:S(2)}) %collective-permute-start.4) | collective-permute-done | bytes 262176 | tf_op jit(solution)/shard_map/ppermute | solution.py:18
  89.3 21.8 %collective-permute-done.20 = f32[2,1,128,256]{3,2,1,0:T(8,128)S(1)} collective-permute-done((f32[2,1,128,256]{3,2,1,0:T(8,128)S(1)}, f32[2,1,128,256]{3,2,1,0:T(8,128)S(1)}, u32[]{:S(2)}, u32[]{:S(2)}) %collective-permute-start.20) | collective-permute-done | bytes 262176 | tf_op jit(solution)/shard_map/ppermute | solution.py:18
  111.4 5.4 %collective-permute-done.10 = f32[2,1,128,256]{3,2,1,0:T(8,128)S(1)} collective-permute-done((f32[2,1,128,256]{3,2,1,0:T(8,128)S(1)}, f32[2,1,128,256]{3,2,1,0:T(8,128)S(1)}, u32[]{:S(2)}, u32[]{:S(2)}) %collective-permute-start.10) | collective-permute-done | bytes 262176 | tf_op jit(solution)/shard_map/ppermute | solution.py:18
  117.1 5.4 %collective-permute-done.5 = f32[2,1,128,256]{3,2,1,0:T(8,128)S(1)} collective-permute-done((f32[2,1,128,256]{3,2,1,0:T(8,128)S(1)}, f32[2,1,128,256]{3,2,1,0:T(8,128)S(1)}, u32[]{:S(2)}, u32[]{:S(2)}) %collective-permute-start.5) | collective-permute-done | bytes 262176 | tf_op jit(solution)/shard_map/ppermute | solution.py:18
  122.9 10.8 %collective-permute-done.11 = f32[2,1,128,256]{3,2,1,0:T(8,128)S(1)} collective-permute-done((f32[2,1,128,256]{3,2,1,0:T(8,128)S(1)}, f32[2,1,128,256]{3,2,1,0:T(8,128)S(1)}, u32[]{:S(2)}, u32[]{:S(2)}) %collective-permute-start.11) | collective-permute-done | bytes 262176 | tf_op jit(solution)/shard_map/ppermute | solution.py:18
  133.8 0.4 fusion.102
  134.2 0.4 fusion.101
  134.8 0.4 fusion.103
  135.2 0.4 fusion.7
  136.5 0.4 fusion.104
  137.0 2.3 collective-permute-done.6
  141.1 0.5 subtract_bitcast_fusion.1
  152.4 1.5 collective-permute-start.12
  154.2 5.5 %collective-permute-done.22 = f32[2,1,128,256]{3,2,1,0:T(8,128)S(1)} collective-permute-done((f32[2,1,128,256]{3,2,1,0:T(8,128)S(1)}, f32[2,1,128,256]{3,2,1,0:T(8,128)S(1)}, u32[]{:S(2)}, u32[]{:S(2)}) %collective-permute-start.22) | collective-permute-done | bytes 262176 | tf_op jit(solution)/shard_map/ppermute | solution.py:18
  159.8 1.3 collective-permute-start.23
  161.1 7.6 %collective-permute-done.12 = f32[2,1,128,256]{3,2,1,0:T(8,128)S(1)} collective-permute-done((f32[2,1,128,256]{3,2,1,0:T(8,128)S(1)}, f32[2,1,128,256]{3,2,1,0:T(8,128)S(1)}, u32[]{:S(2)}, u32[]{:S(2)}) %collective-permute-start.12) | collective-permute-done | bytes 262176 | tf_op jit(solution)/shard_map/ppermute | solution.py:18
  169.3 12.6 %collective-permute-start.24 = (f32[2,1,128,256]{3,2,1,0:T(8,128)S(1)}, f32[2,1,128,256]{3,2,1,0:T(8,128)S(1)}, u32[]{:S(2)}, u32[]{:S(2)}) collective-permute-start(f32[2,1,128,256]{3,2,1,0:T(8,128)S(1)} %fusion.25), channel_id=1, source_target_pairs={{0,4},{4,0},{1,5},{5,1},{2,6},{6,2},{3,7},{7,3},{8,12},{12,8},{9,1... | collective-permute-start | bytes 786440 | tf_op jit(solution)/shard_map/ppermute | solution.py:18
  181.9 2.2 collective-permute-done.13
  184.2 3.4 %collective-permute-start.14 = (f32[2,1,128,256]{3,2,1,0:T(8,128)S(1)}, f32[2,1,128,256]{3,2,1,0:T(8,128)S(1)}, u32[]{:S(2)}, u32[]{:S(2)}) collective-permute-start(f32[2,1,128,256]{3,2,1,0:T(8,128)S(1)} %fusion.21), channel_id=1, source_target_pairs={{0,4},{4,0},{1,5},{5,1},{2,6},{6,2},{3,7},{7,3},{8,12},{12,8},{9,1... | collective-permute-start | bytes 786440 | tf_op jit(solution)/shard_map/ppermute | solution.py:18
  187.8 3.2 %collective-permute-start.25 = (f32[2,1,128,256]{3,2,1,0:T(8,128)S(1)}, f32[2,1,128,256]{3,2,1,0:T(8,128)S(1)}, u32[]{:S(2)}, u32[]{:S(2)}) collective-permute-start(f32[2,1,128,256]{3,2,1,0:T(8,128)S(1)} %fusion.26), channel_id=1, source_target_pairs={{0,8},{8,0},{1,9},{9,1},{2,10},{10,2},{3,11},{11,3},{4,12},{12,4},... | collective-permute-start | bytes 786440 | tf_op jit(solution)/shard_map/ppermute | solution.py:18
  191.0 4.9 %collective-permute-done.14 = f32[2,1,128,256]{3,2,1,0:T(8,128)S(1)} collective-permute-done((f32[2,1,128,256]{3,2,1,0:T(8,128)S(1)}, f32[2,1,128,256]{3,2,1,0:T(8,128)S(1)}, u32[]{:S(2)}, u32[]{:S(2)}) %collective-permute-start.14) | collective-permute-done | bytes 262176 | tf_op jit(solution)/shard_map/ppermute | solution.py:18
  196.0 4.8 %collective-permute-start.15 = (f32[2,1,128,256]{3,2,1,0:T(8,128)S(1)}, f32[2,1,128,256]{3,2,1,0:T(8,128)S(1)}, u32[]{:S(2)}, u32[]{:S(2)}) collective-permute-start(f32[2,1,128,256]{3,2,1,0:T(8,128)S(1)} %fusion.22), channel_id=1, source_target_pairs={{0,8},{8,0},{1,9},{9,1},{2,10},{10,2},{3,11},{11,3},{4,12},{12,4},... | collective-permute-start | bytes 786440 | tf_op jit(solution)/shard_map/ppermute | solution.py:18
  201.1 10.5 %collective-permute-start.26 = (f32[2,1,128,256]{3,2,1,0:T(8,128)S(1)}, f32[2,1,128,256]{3,2,1,0:T(8,128)S(1)}, u32[]{:S(2)}, u32[]{:S(2)}) collective-permute-start(f32[2,1,128,256]{3,2,1,0:T(8,128)S(1)} %fusion.27), channel_id=1, source_target_pairs={{0,16},{16,0},{1,17},{17,1},{2,18},{18,2},{3,19},{19,3},{4,20},{20... | collective-permute-start | bytes 786440 | tf_op jit(solution)/shard_map/ppermute | solution.py:18
  211.7 6.9 %collective-permute-start.16 = (f32[2,1,128,256]{3,2,1,0:T(8,128)S(1)}, f32[2,1,128,256]{3,2,1,0:T(8,128)S(1)}, u32[]{:S(2)}, u32[]{:S(2)}) collective-permute-start(f32[2,1,128,256]{3,2,1,0:T(8,128)S(1)} %fusion.23), channel_id=1, source_target_pairs={{0,16},{16,0},{1,17},{17,1},{2,18},{18,2},{3,19},{19,3},{4,20},{20... | collective-permute-start | bytes 786440 | tf_op jit(solution)/shard_map/ppermute | solution.py:18
  218.7 3.9 %collective-permute-done.26 = f32[2,1,128,256]{3,2,1,0:T(8,128)S(1)} collective-permute-done((f32[2,1,128,256]{3,2,1,0:T(8,128)S(1)}, f32[2,1,128,256]{3,2,1,0:T(8,128)S(1)}, u32[]{:S(2)}, u32[]{:S(2)}) %collective-permute-start.26) | collective-permute-done | bytes 262176 | tf_op jit(solution)/shard_map/ppermute | solution.py:18
  222.6 5.9 %collective-permute-done.16 = f32[2,1,128,256]{3,2,1,0:T(8,128)S(1)} collective-permute-done((f32[2,1,128,256]{3,2,1,0:T(8,128)S(1)}, f32[2,1,128,256]{3,2,1,0:T(8,128)S(1)}, u32[]{:S(2)}, u32[]{:S(2)}) %collective-permute-start.16) | collective-permute-done | bytes 262176 | tf_op jit(solution)/shard_map/ppermute | solution.py:18
  228.7 0.8 fusion.31
  229.5 1.3 collective-permute-start.28
  230.8 4.0 %collective-permute-start.27 = (f32[1,1,256]{2,1,0:T(1,128)S(1)}, f32[1,1,256]{2,1,0:T(1,128)S(1)}, u32[]{:S(2)}, u32[]{:S(2)}) collective-permute-start(f32[1,1,256]{2,1,0:T(1,128)S(1)} %get-tuple-element.99), channel_id=1, source_target_pairs={{0,1},{1,2},{2,3},{3,4},{4,5},{5,6},{6,7},{7,8},{8,9},{9,10},{10,1... | collective-permute-start | bytes 3080 | tf_op jit(solution)/shard_map/ppermute | solution.py:26
  234.8 0.7 slice_bitcast_fusion
  235.5 0.7 fusion.33
  236.2 64.6 %all-reduce.5.cloned.1.call-done = f32[128,256]{1,0:T(8,128)} async-done(((f32[128,256]{1,0:T(8,128)}), f32[128,256]{1,0:T(8,128)}) %all-reduce.5.cloned.1.call-update) | async-done | bytes 131088 | tf_op jit(solution)/shard_map/psum | solution.py:208
  300.8 1.6 copy.220
  (168 shorter events, 17.9 us)
Async XLA Ops:
  7.2 19.5 %copy-start = (bf16[6112,256]{1,0:T(8,128)(2,1)S(1)}, bf16[6112,256]{1,0:T(8,128)(2,1)}, u32[]{:S(2)}) copy-start(bf16[6112,256]{1,0:T(8,128)(2,1)} %param.9) | copy-start | bytes 9388036
  7.2 293.6 %all-reduce.5.cloned.1.call-start = ((), (), s32[]{:S(2)}) async-start(), calls=%async_computation | async-start | bytes 262144 | tf_op jit(solution)/shard_map/psum | solution.py:208
  8.9 27.9 %collective-permute-start.17 = (f32[2,1,128,256]{3,2,1,0:T(8,128)}, f32[2,1,128,256]{3,2,1,0:T(8,128)}, u32[]{:S(2)}, u32[]{:S(2)}) collective-permute-start(f32[2,1,128,256]{3,2,1,0:T(8,128)} %stack.124), channel_id=1, source_target_pairs={{0,16},{16,0},{1,17},{17,1},{2,18},{18,2},{3,19},{19,3},{4,20},{20... | collective-permute-start | bytes 786440 | tf_op jit(solution)/shard_map/ppermute | solution.py:18
  14.1 23.6 %collective-permute-start.7 = (f32[2,1,128,256]{3,2,1,0:T(8,128)}, f32[2,1,128,256]{3,2,1,0:T(8,128)S(1)}, u32[]{:S(2)}, u32[]{:S(2)}) collective-permute-start(f32[2,1,128,256]{3,2,1,0:T(8,128)} %stack.103), channel_id=1, source_target_pairs={{0,16},{16,0},{1,17},{17,1},{2,18},{18,2},{3,19},{19,3},{4,20},{20... | collective-permute-start | bytes 786440 | tf_op jit(solution)/shard_map/ppermute | solution.py:18
  15.4 13.5 %collective-permute-start.1 = (bf16[1,1,256]{2,1,0:T(2,128)(2,1)}, bf16[1,1,256]{2,1,0:T(2,128)(2,1)}, u32[]{:S(2)}, u32[]{:S(2)}) collective-permute-start(bf16[1,1,256]{2,1,0:T(2,128)(2,1)} %get-tuple-element.102), channel_id=1, source_target_pairs={{1,0},{2,1},{3,2},{4,3},{5,4},{6,5},{7,6},{8,7},{9,8},{10,9},{11,1... | collective-permute-start | bytes 1544 | tf_op jit(solution)/shard_map/ppermute | solution.py:29
  16.7 12.3 %collective-permute-start = (bf16[1,1,256]{2,1,0:T(2,128)(2,1)}, bf16[1,1,256]{2,1,0:T(2,128)(2,1)}, u32[]{:S(2)}, u32[]{:S(2)}) collective-permute-start(bf16[1,1,256]{2,1,0:T(2,128)(2,1)} %get-tuple-element.101), channel_id=1, source_target_pairs={{0,1},{1,2},{2,3},{3,4},{4,5},{5,6},{6,7},{7,8},{8,9},{9,10},{10,1... | collective-permute-start | bytes 1544 | tf_op jit(solution)/shard_map/ppermute | solution.py:26
  28.9 11.6 %copy-start.1 = (f32[128,256]{1,0:T(8,128)S(1)}, f32[128,256]{1,0:T(8,128)}, u32[]{:S(2)}) copy-start(f32[128,256]{1,0:T(8,128)} %param.12) | copy-start | bytes 393220
  30.6 11.3 %collective-permute-start.2 = (f32[2,1,128,256]{3,2,1,0:T(8,128)S(1)}, f32[2,1,128,256]{3,2,1,0:T(8,128)S(1)}, u32[]{:S(2)}, u32[]{:S(2)}) collective-permute-start(f32[2,1,128,256]{3,2,1,0:T(8,128)S(1)} %stack.97), channel_id=1, source_target_pairs={{0,16},{16,0},{1,17},{17,1},{2,18},{18,2},{3,19},{19,3},{4,20},{20... | collective-permute-start | bytes 786440 | tf_op jit(solution)/shard_map/ppermute | solution.py:18
  39.8 8.5 %collective-permute-start.18 = (f32[2,1,128,256]{3,2,1,0:T(8,128)S(1)}, f32[2,1,128,256]{3,2,1,0:T(8,128)S(1)}, u32[]{:S(2)}, u32[]{:S(2)}) collective-permute-start(f32[2,1,128,256]{3,2,1,0:T(8,128)S(1)} %maximum_select_fusion.10), channel_id=1, source_target_pairs={{0,8},{8,0},{1,9},{9,1},{2,10},{10,2},{3,11},{11,3},{4,12},{12,4},... | collective-permute-start | bytes 786440 | tf_op jit(solution)/shard_map/ppermute | solution.py:18
  40.5 13.4 %collective-permute-start.8 = (f32[2,1,128,256]{3,2,1,0:T(8,128)S(1)}, f32[2,1,128,256]{3,2,1,0:T(8,128)S(1)}, u32[]{:S(2)}, u32[]{:S(2)}) collective-permute-start(f32[2,1,128,256]{3,2,1,0:T(8,128)S(1)} %maximum_select_fusion.5), channel_id=1, source_target_pairs={{0,8},{8,0},{1,9},{9,1},{2,10},{10,2},{3,11},{11,3},{4,12},{12,4},... | collective-permute-start | bytes 786440 | tf_op jit(solution)/shard_map/ppermute | solution.py:18
  42.0 17.5 %collective-permute-start.3 = (f32[2,1,128,256]{3,2,1,0:T(8,128)S(1)}, f32[2,1,128,256]{3,2,1,0:T(8,128)S(1)}, u32[]{:S(2)}, u32[]{:S(2)}) collective-permute-start(f32[2,1,128,256]{3,2,1,0:T(8,128)S(1)} %maximum_select_fusion), channel_id=1, source_target_pairs={{0,8},{8,0},{1,9},{9,1},{2,10},{10,2},{3,11},{11,3},{4,12},{12,4},... | collective-permute-start | bytes 786440 | tf_op jit(solution)/shard_map/ppermute | solution.py:18
  50.4 13.4 %collective-permute-start.19 = (f32[2,1,128,256]{3,2,1,0:T(8,128)S(1)}, f32[2,1,128,256]{3,2,1,0:T(8,128)S(1)}, u32[]{:S(2)}, u32[]{:S(2)}) collective-permute-start(f32[2,1,128,256]{3,2,1,0:T(8,128)S(1)} %maximum_select_fusion.11), channel_id=1, source_target_pairs={{0,4},{4,0},{1,5},{5,1},{2,6},{6,2},{3,7},{7,3},{8,12},{12,8},{9,1... | collective-permute-start | bytes 786440 | tf_op jit(solution)/shard_map/ppermute | solution.py:18
  54.1 24.2 %collective-permute-start.9 = (f32[2,1,128,256]{3,2,1,0:T(8,128)S(1)}, f32[2,1,128,256]{3,2,1,0:T(8,128)S(1)}, u32[]{:S(2)}, u32[]{:S(2)}) collective-permute-start(f32[2,1,128,256]{3,2,1,0:T(8,128)S(1)} %maximum_select_fusion.6), channel_id=1, source_target_pairs={{0,4},{4,0},{1,5},{5,1},{2,6},{6,2},{3,7},{7,3},{8,12},{12,8},{9,1... | collective-permute-start | bytes 786440 | tf_op jit(solution)/shard_map/ppermute | solution.py:18
  59.7 29.4 %collective-permute-start.4 = (f32[2,1,128,256]{3,2,1,0:T(8,128)S(1)}, f32[2,1,128,256]{3,2,1,0:T(8,128)S(1)}, u32[]{:S(2)}, u32[]{:S(2)}) collective-permute-start(f32[2,1,128,256]{3,2,1,0:T(8,128)S(1)} %maximum_select_fusion.1), channel_id=1, source_target_pairs={{0,4},{4,0},{1,5},{5,1},{2,6},{6,2},{3,7},{7,3},{8,12},{12,8},{9,1... | collective-permute-start | bytes 786440 | tf_op jit(solution)/shard_map/ppermute | solution.py:18
  64.0 47.2 %collective-permute-start.20 = (f32[2,1,128,256]{3,2,1,0:T(8,128)S(1)}, f32[2,1,128,256]{3,2,1,0:T(8,128)S(1)}, u32[]{:S(2)}, u32[]{:S(2)}) collective-permute-start(f32[2,1,128,256]{3,2,1,0:T(8,128)S(1)} %maximum_select_fusion.12), channel_id=1, source_target_pairs={{0,2},{2,0},{1,3},{3,1},{4,6},{6,4},{5,7},{7,5},{8,10},{10,8},{9,1... | collective-permute-start | bytes 786440 | tf_op jit(solution)/shard_map/ppermute | solution.py:18
  78.4 38.4 %collective-permute-start.10 = (f32[2,1,128,256]{3,2,1,0:T(8,128)S(1)}, f32[2,1,128,256]{3,2,1,0:T(8,128)S(1)}, u32[]{:S(2)}, u32[]{:S(2)}) collective-permute-start(f32[2,1,128,256]{3,2,1,0:T(8,128)S(1)} %maximum_select_fusion.7), channel_id=1, source_target_pairs={{0,2},{2,0},{1,3},{3,1},{4,6},{6,4},{5,7},{7,5},{8,10},{10,8},{9,1... | collective-permute-start | bytes 786440 | tf_op jit(solution)/shard_map/ppermute | solution.py:18
  89.2 33.2 %collective-permute-start.5 = (f32[2,1,128,256]{3,2,1,0:T(8,128)S(1)}, f32[2,1,128,256]{3,2,1,0:T(8,128)S(1)}, u32[]{:S(2)}, u32[]{:S(2)}) collective-permute-start(f32[2,1,128,256]{3,2,1,0:T(8,128)S(1)} %maximum_select_fusion.2), channel_id=1, source_target_pairs={{0,2},{2,0},{1,3},{3,1},{4,6},{6,4},{5,7},{7,5},{8,10},{10,8},{9,1... | collective-permute-start | bytes 786440 | tf_op jit(solution)/shard_map/ppermute | solution.py:18
  111.3 23.3 %collective-permute-start.21 = (f32[2,1,128,256]{3,2,1,0:T(8,128)S(1)}, f32[2,1,128,256]{3,2,1,0:T(8,128)S(1)}, u32[]{:S(2)}, u32[]{:S(2)}) collective-permute-start(f32[2,1,128,256]{3,2,1,0:T(8,128)S(1)} %maximum_select_fusion.13), channel_id=1, source_target_pairs={{0,1},{1,0},{2,3},{3,2},{4,5},{5,4},{6,7},{7,6},{8,9},{9,8},{10,11... | collective-permute-start | bytes 786440 | tf_op jit(solution)/shard_map/ppermute | solution.py:18
  117.0 16.7 %collective-permute-start.11 = (f32[2,1,128,256]{3,2,1,0:T(8,128)S(1)}, f32[2,1,128,256]{3,2,1,0:T(8,128)S(1)}, u32[]{:S(2)}, u32[]{:S(2)}) collective-permute-start(f32[2,1,128,256]{3,2,1,0:T(8,128)S(1)} %maximum_select_fusion.8), channel_id=1, source_target_pairs={{0,1},{1,0},{2,3},{3,2},{4,5},{5,4},{6,7},{7,6},{8,9},{9,8},{10,11... | collective-permute-start | bytes 786440 | tf_op jit(solution)/shard_map/ppermute | solution.py:18
  122.6 16.7 %collective-permute-start.6 = (f32[2,1,128,256]{3,2,1,0:T(8,128)S(1)}, f32[2,1,128,256]{3,2,1,0:T(8,128)S(1)}, u32[]{:S(2)}, u32[]{:S(2)}) collective-permute-start(f32[2,1,128,256]{3,2,1,0:T(8,128)S(1)} %maximum_select_fusion.3), channel_id=1, source_target_pairs={{0,1},{1,0},{2,3},{3,2},{4,5},{5,4},{6,7},{7,6},{8,9},{9,8},{10,11... | collective-permute-start | bytes 786440 | tf_op jit(solution)/shard_map/ppermute | solution.py:18
  135.7 5.4 %copy-start.3 = (f32[8,16]{0,1:T(8,128)S(1)}, f32[8,16]{0,1:T(8,128)}, u32[]{:S(2)}) copy-start(f32[8,16]{0,1:T(8,128)} %get-tuple-element.125) | copy-start | bytes 1540
  135.7 5.4 %copy-start.4 = (f32[8,16]{0,1:T(8,128)S(1)}, f32[8,16]{0,1:T(8,128)}, u32[]{:S(2)}) copy-start(f32[8,16]{0,1:T(8,128)} %get-tuple-element.126) | copy-start | bytes 1540
  146.2 5.4 %copy-start.9 = (f32[128]{0:T(128)S(1)}, f32[128]{0:T(128)}, u32[]{:S(2)}) copy-start(f32[128]{0:T(128)} %get-tuple-element.121) | copy-start | bytes 1540
  146.2 5.4 %copy-start.10 = (f32[128]{0:T(128)S(1)}, f32[128]{0:T(128)}, u32[]{:S(2)}) copy-start(f32[128]{0:T(128)} %get-tuple-element.122) | copy-start | bytes 1540
  152.0 7.7 %collective-permute-start.22 = (f32[2,1,128,256]{3,2,1,0:T(8,128)S(1)}, f32[2,1,128,256]{3,2,1,0:T(8,128)S(1)}, u32[]{:S(2)}, u32[]{:S(2)}) collective-permute-start(f32[2,1,128,256]{3,2,1,0:T(8,128)S(1)} %pad_maximum_fusion.1), channel_id=1, source_target_pairs={{0,1},{1,0},{2,3},{3,2},{4,5},{5,4},{6,7},{7,6},{8,9},{9,8},{10,11... | collective-permute-start | bytes 786440 | tf_op jit(solution)/shard_map/ppermute | solution.py:18
  152.4 16.4 %collective-permute-start.12 = (f32[2,1,128,256]{3,2,1,0:T(8,128)S(1)}, f32[2,1,128,256]{3,2,1,0:T(8,128)S(1)}, u32[]{:S(2)}, u32[]{:S(2)}) collective-permute-start(f32[2,1,128,256]{3,2,1,0:T(8,128)S(1)} %pad_maximum_fusion), channel_id=1, source_target_pairs={{0,1},{1,0},{2,3},{3,2},{4,5},{5,4},{6,7},{7,6},{8,9},{9,8},{10,11... | collective-permute-start | bytes 786440 | tf_op jit(solution)/shard_map/ppermute | solution.py:18
  159.8 9.3 %collective-permute-start.23 = (f32[2,1,128,256]{3,2,1,0:T(8,128)S(1)}, f32[2,1,128,256]{3,2,1,0:T(8,128)S(1)}, u32[]{:S(2)}, u32[]{:S(2)}) collective-permute-start(f32[2,1,128,256]{3,2,1,0:T(8,128)S(1)} %fusion.24), channel_id=1, source_target_pairs={{0,2},{2,0},{1,3},{3,1},{4,6},{6,4},{5,7},{7,5},{8,10},{10,8},{9,1... | collective-permute-start | bytes 786440 | tf_op jit(solution)/shard_map/ppermute | solution.py:18
  168.9 15.2 %collective-permute-start.13 = (f32[2,1,128,256]{3,2,1,0:T(8,128)S(1)}, f32[2,1,128,256]{3,2,1,0:T(8,128)S(1)}, u32[]{:S(2)}, u32[]{:S(2)}) collective-permute-start(f32[2,1,128,256]{3,2,1,0:T(8,128)S(1)} %fusion.20), channel_id=1, source_target_pairs={{0,2},{2,0},{1,3},{3,1},{4,6},{6,4},{5,7},{7,5},{8,10},{10,8},{9,1... | collective-permute-start | bytes 786440 | tf_op jit(solution)/shard_map/ppermute | solution.py:18
  169.3 18.4 %collective-permute-start.24 = (f32[2,1,128,256]{3,2,1,0:T(8,128)S(1)}, f32[2,1,128,256]{3,2,1,0:T(8,128)S(1)}, u32[]{:S(2)}, u32[]{:S(2)}) collective-permute-start(f32[2,1,128,256]{3,2,1,0:T(8,128)S(1)} %fusion.25), channel_id=1, source_target_pairs={{0,4},{4,0},{1,5},{5,1},{2,6},{6,2},{3,7},{7,3},{8,12},{12,8},{9,1... | collective-permute-start | bytes 786440 | tf_op jit(solution)/shard_map/ppermute | solution.py:18
  184.2 11.7 %collective-permute-start.14 = (f32[2,1,128,256]{3,2,1,0:T(8,128)S(1)}, f32[2,1,128,256]{3,2,1,0:T(8,128)S(1)}, u32[]{:S(2)}, u32[]{:S(2)}) collective-permute-start(f32[2,1,128,256]{3,2,1,0:T(8,128)S(1)} %fusion.21), channel_id=1, source_target_pairs={{0,4},{4,0},{1,5},{5,1},{2,6},{6,2},{3,7},{7,3},{8,12},{12,8},{9,1... | collective-permute-start | bytes 786440 | tf_op jit(solution)/shard_map/ppermute | solution.py:18
  187.8 13.1 %collective-permute-start.25 = (f32[2,1,128,256]{3,2,1,0:T(8,128)S(1)}, f32[2,1,128,256]{3,2,1,0:T(8,128)S(1)}, u32[]{:S(2)}, u32[]{:S(2)}) collective-permute-start(f32[2,1,128,256]{3,2,1,0:T(8,128)S(1)} %fusion.26), channel_id=1, source_target_pairs={{0,8},{8,0},{1,9},{9,1},{2,10},{10,2},{3,11},{11,3},{4,12},{12,4},... | collective-permute-start | bytes 786440 | tf_op jit(solution)/shard_map/ppermute | solution.py:18
  196.0 15.6 %collective-permute-start.15 = (f32[2,1,128,256]{3,2,1,0:T(8,128)S(1)}, f32[2,1,128,256]{3,2,1,0:T(8,128)S(1)}, u32[]{:S(2)}, u32[]{:S(2)}) collective-permute-start(f32[2,1,128,256]{3,2,1,0:T(8,128)S(1)} %fusion.22), channel_id=1, source_target_pairs={{0,8},{8,0},{1,9},{9,1},{2,10},{10,2},{3,11},{11,3},{4,12},{12,4},... | collective-permute-start | bytes 786440 | tf_op jit(solution)/shard_map/ppermute | solution.py:18
  200.9 27.7 %copy-start.2 = (bf16[1,128,256]{2,1,0:T(8,128)(2,1)S(1)}, bf16[1,128,256]{2,1,0:T(8,128)(2,1)}, u32[]{:S(2)}) copy-start(bf16[1,128,256]{2,1,0:T(8,128)(2,1)} %param.13) | copy-start | bytes 196612
  201.0 27.7 %copy-start.5 = (f32[1,256]{1,0:T(1,128)S(1)}, f32[1,256]{1,0:T(1,128)}, u32[]{:S(2)}) copy-start(f32[1,256]{1,0:T(1,128)} %get-tuple-element.109) | copy-start | bytes 3076
  201.0 27.7 %copy-start.6 = (f32[1,256]{1,0:T(1,128)S(1)}, f32[1,256]{1,0:T(1,128)}, u32[]{:S(2)}) copy-start(f32[1,256]{1,0:T(1,128)} %get-tuple-element.110) | copy-start | bytes 3076
  201.0 27.7 %copy-start.7 = (f32[1,256]{1,0:T(1,128)S(1)}, f32[1,256]{1,0:T(1,128)}, u32[]{:S(2)}) copy-start(f32[1,256]{1,0:T(1,128)} %get-tuple-element.111) | copy-start | bytes 3076
  201.0 27.7 %copy-start.8 = (f32[1,256]{1,0:T(1,128)S(1)}, f32[1,256]{1,0:T(1,128)}, u32[]{:S(2)}) copy-start(f32[1,256]{1,0:T(1,128)} %fusion.428) | copy-start | bytes 3076
  201.0 27.7 %copy-start.11 = (f32[256]{0:T(256)S(1)}, f32[256]{0:T(256)}, u32[]{:S(2)}) copy-start(f32[256]{0:T(256)} %param.11) | copy-start | bytes 3076
  201.1 21.5 %collective-permute-start.26 = (f32[2,1,128,256]{3,2,1,0:T(8,128)S(1)}, f32[2,1,128,256]{3,2,1,0:T(8,128)S(1)}, u32[]{:S(2)}, u32[]{:S(2)}) collective-permute-start(f32[2,1,128,256]{3,2,1,0:T(8,128)S(1)} %fusion.27), channel_id=1, source_target_pairs={{0,16},{16,0},{1,17},{17,1},{2,18},{18,2},{3,19},{19,3},{4,20},{20... | collective-permute-start | bytes 786440 | tf_op jit(solution)/shard_map/ppermute | solution.py:18
  211.7 16.8 %collective-permute-start.16 = (f32[2,1,128,256]{3,2,1,0:T(8,128)S(1)}, f32[2,1,128,256]{3,2,1,0:T(8,128)S(1)}, u32[]{:S(2)}, u32[]{:S(2)}) collective-permute-start(f32[2,1,128,256]{3,2,1,0:T(8,128)S(1)} %fusion.23), channel_id=1, source_target_pairs={{0,16},{16,0},{1,17},{17,1},{2,18},{18,2},{3,19},{19,3},{4,20},{20... | collective-permute-start | bytes 786440 | tf_op jit(solution)/shard_map/ppermute | solution.py:18
  229.5 6.0 %collective-permute-start.28 = (f32[1,1,256]{2,1,0:T(1,128)S(1)}, f32[1,1,256]{2,1,0:T(1,128)S(1)}, u32[]{:S(2)}, u32[]{:S(2)}) collective-permute-start(f32[1,1,256]{2,1,0:T(1,128)S(1)} %get-tuple-element.100), channel_id=1, source_target_pairs={{1,0},{2,1},{3,2},{4,3},{5,4},{6,5},{7,6},{8,7},{9,8},{10,9},{11,1... | collective-permute-start | bytes 3080 | tf_op jit(solution)/shard_map/ppermute | solution.py:29
  230.8 4.7 %collective-permute-start.27 = (f32[1,1,256]{2,1,0:T(1,128)S(1)}, f32[1,1,256]{2,1,0:T(1,128)S(1)}, u32[]{:S(2)}, u32[]{:S(2)}) collective-permute-start(f32[1,1,256]{2,1,0:T(1,128)S(1)} %get-tuple-element.99), channel_id=1, source_target_pairs={{0,1},{1,2},{2,3},{3,4},{4,5},{5,6},{6,7},{7,8},{8,9},{9,10},{10,1... | collective-permute-start | bytes 3080 | tf_op jit(solution)/shard_map/ppermute | solution.py:26
Sparse Core Ops, SparseCore 0:
  235.6 65.1 all-reduce.4
where the time goes:
time: 311 us; the launch traced here: 309 us
  waiting for transfers between devices  175 us (56%)
  starting transfers between devices  78.3 us (25%)
  between operations  17.1 us (5%)
  matrix products  16 us (5%)
  other arithmetic  14.3 us (5%)
  local copies, waits for them, and re-layouts  8.5 us (3%)
    ppermute x25, waiting for transfers between devices, from_partner(): return lax.ppermute(block, axis, route)  110 us
    ppermute x25, starting transfers between devices, from_partner(): return lax.ppermute(block, axis, route)  66.8 us
    psum x1, waiting for transfers between devices, local(): filter_grad = lax.psum(restored[1][0], 'dp')  64.6 us
    ppermute x2, starting transfers between devices, with_halo(): lax.ppermute(lax.slice_in_dim(block, block.shape[dim] - width, None, axis...  8.97 us
    dot_general x20, matrix products, outer_mix(): jnp.einsum('ka,bamc->bkmc', matrix_table, field_data, precision=PRECISE)  7.75 us
    dot_general x20, matrix products, inner_mix(): jnp.einsum('qm,bkmc->bqkc', matrix_table, field_data, precision=PRECISE)  6.44 us
  transfers between devices with their start and end apart: 30, of which 20 were waited for; matrix products, arithmetic and copies ran while one was open for 7% of the time, Pallas kernels for 0%

commit v1 on v0

v1 whole, which is shorter than its diff:
```python
import functools
import math

import jax
import jax.numpy as jnp
import ml_dtypes
import numpy as np
from jax import lax
from jax.experimental import pallas as pl
from jax.experimental.pallas import tpu as pltpu
from jax.sharding import PartitionSpec as P

MESH = pl.DeviceIdType.MESH
F32 = jnp.float32
BF16 = jnp.bfloat16
PACK = 8
ROWS16 = 16


def halves(array):
    high = array.astype(ml_dtypes.bfloat16)
    low = (array - high.astype(np.float64)).astype(ml_dtypes.bfloat16)
    return high, low


def make_tables(blocks, samples):
    total = blocks * samples
    index = np.arange(blocks)
    angle = 2.0 * math.pi / blocks * (np.outer(index, index) % blocks)
    spread = np.eye(PACK)
    left = np.concatenate([np.kron(np.cos(angle), spread), -np.kron(np.sin(angle), spread)])
    inner = np.arange(samples)
    angle = 2.0 * math.pi / samples * (np.outer(inner, inner) % samples)
    right = np.block([[np.cos(angle), -np.sin(angle)], [np.sin(angle), np.cos(angle)]])
    turn = 2.0 * math.pi / total * np.outer(index, inner)
    turn = np.repeat(turn, PACK, axis=0)
    return (
        *halves(left),
        *halves(right),
        np.cos(turn).astype(np.float32),
        np.sin(turn).astype(np.float32),
    )


def split(array):
    high = array.astype(BF16)
    return high, (array - high.astype(F32)).astype(BF16)


def dot(a, b):
    return jnp.dot(a, b, preferred_element_type=F32)


def stencil(field, taps):
    lanes = field.shape[2]
    lane = lax.broadcasted_iota(jnp.int32, field.shape, 2)
    edge = jnp.zeros((1,) + field.shape[1:], F32)
    turned = pltpu.roll(field, 1, 2)
    before = jnp.where(lane == 0, jnp.concatenate([edge, turned[:-1]], axis=0), turned)
    turned = pltpu.roll(field, lanes - 1, 2)
    after = jnp.where(lane == lanes - 1, jnp.concatenate([turned[1:], edge], axis=0), turned)
    return taps[0] * before + taps[1] * field + taps[2] * after


def kernel(
    tm_size,
    dp_size,
    ids_ref,
    wave_ref,
    cot_ref,
    filt_ref,
    taps_ref,
    gain_ref,
    speakers_hbm,
    lh_hbm,
    ll_hbm,
    rh_hbm,
    rl_hbm,
    tc_hbm,
    ts_hbm,
    layer_ref,
    gradw_ref,
    fgrad_ref,
    speakers,
    lh,
    ll,
    rh,
    rl,
    tc,
    ts,
    send_a,
    recv_a,
    send_f,
    recv_f,
    send_c,
    recv_c,
    send_r,
    recv_r,
    send_g,
    recv_g,
    local_sem,
    send_sem,
    recv_sem,
):
    dp = lax.axis_index("dp")
    tm = lax.axis_index("tm")
    per = tm_size // dp_size
    samples = wave_ref.shape[0]
    channels = wave_ref.shape[1]
    rows = tm_size * PACK

    barrier = pltpu.get_barrier_semaphore()

    @pl.loop(1, tm_size)
    def _(step):
        pl.semaphore_signal(
            barrier, inc=1, device_id=(dp, lax.rem(tm + step, tm_size)), device_id_type=MESH
        )

    @pl.loop(1, dp_size)
    def _(step):
        pl.semaphore_signal(
            barrier, inc=1, device_id=(lax.rem(dp + step, dp_size), tm), device_id_type=MESH
        )

    loads = [
        pltpu.make_async_copy(source, target, local_sem.at[place])
        for place, (source, target) in enumerate(
            [
                (lh_hbm, lh),
                (ll_hbm, ll),
                (rh_hbm, rh),
                (rl_hbm, rl),
                (tc_hbm, tc),
                (ts_hbm, ts),
                (speakers_hbm, speakers),
            ]
        )
    ]
    for load in loads:
        load.start()

    wave_t = wave_ref[...].astype(F32).T.reshape(tm_size, PACK, samples)
    cot_t = cot_ref[...].astype(F32).T.reshape(tm_size, PACK, samples)
    send_a[...] = jnp.concatenate([wave_t, cot_t], axis=1).astype(BF16)
    send_f[...] = filt_ref[...].T.reshape(tm_size, PACK, samples)

    def exchange(source, target, which):
        @pl.loop(1, tm_size)
        def _(step):
            peer = lax.rem(tm + step, tm_size)
            pltpu.make_async_remote_copy(
                src_ref=source.at[peer],
                dst_ref=target.at[tm],
                send_sem=send_sem.at[which],
                recv_sem=recv_sem.at[which],
                device_id=(dp, peer),
                device_id_type=MESH,
            ).start()

        target[tm] = source[tm]

    def wait_bytes(like, sem):
        pltpu.make_async_copy(like, like, sem).wait()

    pl.semaphore_wait(barrier, tm_size - 1 + dp_size - 1)
    exchange(send_a, recv_a, 0)
    exchange(send_f, recv_f, 1)

    for load in loads:
        load.wait()
    lane = lax.broadcasted_iota(jnp.int32, (PACK, channels), 1)
    row = lax.broadcasted_iota(jnp.int32, (PACK, channels), 0)
    mine = lane == tm * PACK + row

    def column(vector):
        return jnp.sum(jnp.where(mine, vector, 0.0), axis=1, keepdims=True)

    speaker = ids_ref[0]
    group = speakers[lax.div(speaker, ROWS16)]
    picked = lax.broadcasted_iota(jnp.int32, (ROWS16, channels), 0) == lax.rem(speaker, ROWS16)
    speaker_row = jnp.sum(jnp.where(picked, group.astype(F32), 0.0), axis=0, keepdims=True)
    scale = column(speaker_row)
    taps = [column(taps_ref[place : place + 1, :]) for place in range(3)]
    gain = column(gain_ref[...])

    def left_mix(field):
        high, low = split(field)
        return dot(lh[...], high) + (dot(ll[...], high) + dot(lh[...], low))

    def right_mix(field):
        high, low = split(field)
        return dot(high, rh[...]) + (dot(high, rl[...]) + dot(low, rh[...]))

    def twiddle(real, imag):
        return real * tc[...] + imag * ts[...], imag * tc[...] - real * ts[...]

    def forward(fields):
        mixed = left_mix(jnp.concatenate(fields, axis=1))
        turned = []
        for place in range(len(fields)):
            at = slice(place * samples, (place + 1) * samples)
            turned.append(jnp.concatenate(twiddle(mixed[:rows, at], mixed[rows:, at]), axis=1))
        result = right_mix(jnp.concatenate(turned, axis=0))
        return [
            (
                result[place * rows : (place + 1) * rows, :samples],
                result[place * rows : (place + 1) * rows, samples:],
            )
            for place in range(len(fields))
        ]

    def to_blocks(field):
        return field.reshape(tm_size, PACK, samples)

    wait_bytes(recv_a.at[pl.ds(0, tm_size - 1)], recv_sem.at[0])
    both = recv_a[...].astype(F32)
    value = stencil(both[:, :PACK], taps) * scale
    grad = both[:, PACK:]
    (vr, vi), (gr, gi) = forward([value.reshape(rows, samples), grad.reshape(rows, samples)])

    inverse_scale = 1.0 / (tm_size * samples)
    term_r = (vr * gr + vi * gi) * inverse_scale
    term_i = (vr * gi - vi * gr) * inverse_scale
    inner = right_mix(jnp.concatenate([term_r, -term_i], axis=1))
    inner_r, inner_i = twiddle(inner[:, :samples], inner[:, samples:])
    high_r, low_r = split(inner_r)
    high_i, low_i = split(inner_i)
    partial = (
        dot(lh[:rows, :], high_r)
        + dot(ll[:rows, :], high_r)
        + dot(lh[:rows, :], low_r)
        - dot(lh[rows:, :], high_i)
        - dot(ll[rows:, :], high_i)
        - dot(lh[rows:, :], low_i)
    )
    send_r[...] = partial.reshape(dp_size, per * PACK, samples)

    @pl.loop(1, dp_size)
    def _(step):
        peer = lax.rem(dp + step, dp_size)
        pltpu.make_async_remote_copy(
            src_ref=send_r.at[peer],
            dst_ref=recv_r.at[dp],
            send_sem=send_sem.at[2],
            recv_sem=recv_sem.at[2],
            device_id=(peer, tm),
            device_id_type=MESH,
        ).start()

    recv_r[dp] = send_r[dp]

    wait_bytes(recv_f.at[pl.ds(0, tm_size - 1)], recv_sem.at[1])
    ((fr, fi),) = forward([recv_f[...].reshape(rows, samples)])
    fr = fr * inverse_scale
    fi = fi * inverse_scale
    pr = vr * fr - vi * fi
    pi = vr * fi + vi * fr
    qr = gr * fr + gi * fi
    qi = gi * fr - gr * fi
    inner = right_mix(jnp.concatenate([pr - qi, -(pi + qr)], axis=1))
    inner = jnp.concatenate(twiddle(inner[:, :samples], inner[:, samples:]), axis=1)
    mixed = left_mix(inner)
    convolved = mixed[:rows, :samples] - mixed[rows:, samples:]
    correlated = -mixed[rows:, :samples] - mixed[:rows, samples:]

    layer = to_blocks(convolved) + gain * value
    middle = (to_blocks(correlated) + gain * grad) * scale
    send_c[...] = jnp.concatenate([layer, stencil(middle, taps[::-1])], axis=1)
    exchange(send_c, recv_c, 3)

    wait_bytes(recv_r.at[pl.ds(0, dp_size - 1)], recv_sem.at[2])
    total = recv_r[0]
    for place in range(1, dp_size):
        total = total + recv_r[place]
    send_g[...] = total.reshape(per, PACK, samples)
    own = tm // per == dp

    @pl.loop(0, tm_size)
    def _(step):
        place = step // dp_size
        peer_dp = lax.rem(dp + step, dp_size)
        peer_tm = dp * per + place
        itself = (peer_dp == dp) & (peer_tm == tm)

        @pl.when(jnp.logical_not(itself))
        def _():
            pltpu.make_async_remote_copy(
                src_ref=send_g.at[place],
                dst_ref=recv_g.at[tm],
                send_sem=send_sem.at[4],
                recv_sem=recv_sem.at[4],
                device_id=(peer_dp, peer_tm),
                device_id_type=MESH,
            ).start()

        @pl.when(itself)
        def _():
            recv_g[tm] = send_g[place]

    wait_bytes(recv_c.at[pl.ds(0, tm_size - 1)], recv_sem.at[3])
    layer_ref[...] = recv_c[:, :PACK, :].reshape(rows, samples).T
    gradw_ref[...] = recv_c[:, PACK:, :].reshape(rows, samples).T

    @pl.when(own)
    def _():
        wait_bytes(recv_g.at[pl.ds(0, tm_size - 1)], recv_sem.at[4])

    @pl.when(jnp.logical_not(own))
    def _():
        wait_bytes(recv_g, recv_sem.at[4])

    fgrad_ref[...] = recv_g[...].reshape(rows, samples).T

    wait_bytes(send_a.at[pl.ds(0, tm_size - 1)], send_sem.at[0])
    wait_bytes(send_f.at[pl.ds(0, tm_size - 1)], send_sem.at[1])
    wait_bytes(send_r.at[pl.ds(0, dp_size - 1)], send_sem.at[2])
    wait_bytes(send_c.at[pl.ds(0, tm_size - 1)], send_sem.at[3])

    @pl.when(own)
    def _():
        wait_bytes(recv_g.at[pl.ds(0, tm_size - 1)], send_sem.at[4])

    @pl.when(jnp.logical_not(own))
    def _():
        wait_bytes(recv_g, send_sem.at[4])


def local(waveform, speaker_ids, speaker_table, stencil_taps, skip_gain, filters, cotangent):
    tm_size, dp_size = lax.axis_size("tm"), lax.axis_size("dp")
    samples, channels = filters.shape
    per = tm_size // dp_size
    rows = tm_size * PACK
    tables = make_tables(tm_size, samples)
    vmem = pl.BlockSpec(memory_space=pltpu.VMEM)
    anywhere = pl.BlockSpec(memory_space=pl.ANY)
    block = jax.ShapeDtypeStruct((samples, channels), F32)
    layer_out, grad_waveform, filter_grad = pl.pallas_call(
        functools.partial(kernel, tm_size, dp_size),
        out_shape=[block, block, block],
        in_specs=[pl.BlockSpec(memory_space=pltpu.SMEM)] + [vmem] * 5 + [anywhere] * 7,
        out_specs=[vmem] * 3,
        scratch_shapes=[
            pltpu.VMEM((speaker_table.shape[0] // ROWS16, ROWS16, channels), BF16),
            *[pltpu.VMEM(table.shape, table.dtype) for table in tables],
            pltpu.VMEM((tm_size, 2 * PACK, samples), BF16),
            pltpu.VMEM((tm_size, 2 * PACK, samples), BF16),
            pltpu.VMEM((tm_size, PACK, samples), F32),
            pltpu.VMEM((tm_size, PACK, samples), F32),
            pltpu.VMEM((tm_size, 2 * PACK, samples), F32),
            pltpu.VMEM((tm_size, 2 * PACK, samples), F32),
            pltpu.VMEM((dp_size, per * PACK, samples), F32),
            pltpu.VMEM((dp_size, per * PACK, samples), F32),
            pltpu.VMEM((per, PACK, samples), F32),
            pltpu.VMEM((tm_size, PACK, samples), F32),
            pltpu.SemaphoreType.DMA((7,)),
            pltpu.SemaphoreType.DMA((5,)),
            pltpu.SemaphoreType.DMA((5,)),
        ],
        compiler_params=pltpu.CompilerParams(
            collective_id=0, has_side_effects=True, vmem_limit_bytes=40 * 1024 * 1024
        ),
    )(
        speaker_ids,
        waveform[0],
        cotangent[0],
        filters,
        stencil_taps,
        skip_gain[None],
        speaker_table.reshape(-1, ROWS16, channels),
        *[jnp.asarray(table) for table in tables],
    )
    return layer_out[None], grad_waveform[None], filter_grad


def solution(mesh):
    return jax.shard_map(
        local,
        mesh=mesh,
        in_specs=(P("dp", "tm", None), P("dp"), P(), P(), P(), P("tm", None), P("dp", "tm", None)),
        out_specs=(P("dp", "tm", None), P("dp", "tm", None), P("tm", None)),
        check_vma=False,
    )
```

time: 311 us -> 48.9 us (0.16)
  the two profiles are of different devices: /device:TPU:1 before, /device:TPU:7 now
where the time goes in v1:
time: 48.9 us; the launch traced here: 48.5 us
  Pallas kernels  33.9 us (69%)
  local copies, waits for them, and re-layouts  13.3 us (27%)
  between operations  1.31 us (3%)
    pallas_call x1, Pallas kernels, local(): pl.pallas_call(functools.partial(kernel, tm_size, dp_size), out_shape=[bl...  33.9 us
    unnamed x27, local copies, waits for them, and re-layouts  13.3 us

profile of v1, /device:TPU:7, one launch (start us, length us, event | category | flops | bytes accessed | tf_op | source)
XLA Modules:
  0.0 48.5 jit_solution(2578941178703603825)
XLA Ops:
  1.3 0.0 copy-start
  1.3 1.9 %copy-done = bf16[6112,256]{1,0:T(8,128)(2,1)S(1)} copy-done((bf16[6112,256]{1,0:T(8,128)(2,1)S(1)}, bf16[6112,256]{1,0:T(8,128)(2,1)}, u32[]{:S(2)}) %copy-start) | copy-done | bytes 3129368
  3.2 0.0 copy-start.1
  3.2 0.9 %copy-done.1 = bf16[512,256]{1,0:T(8,128)(2,1)S(1)} copy-done((bf16[512,256]{1,0:T(8,128)(2,1)S(1)}, bf16[512,256]{1,0:T(8,128)(2,1)}, u32[]{:S(2)}) %copy-start.1) | copy-done | bytes 262168
  4.1 0.0 copy-start.2
  4.1 0.9 %copy-done.2 = bf16[512,256]{1,0:T(8,128)(2,1)S(1)} copy-done((bf16[512,256]{1,0:T(8,128)(2,1)S(1)}, bf16[512,256]{1,0:T(8,128)(2,1)}, u32[]{:S(2)}) %copy-start.2) | copy-done | bytes 262168
  5.1 0.0 copy-start.3
  5.1 0.9 %copy-done.3 = f32[128,256]{1,0:T(8,128)S(1)} copy-done((f32[128,256]{1,0:T(8,128)S(1)}, f32[128,256]{1,0:T(8,128)}, u32[]{:S(2)}) %copy-start.3) | copy-done | bytes 131096
  6.0 0.0 copy-start.4
  6.0 0.9 %copy-done.4 = f32[256,128]{1,0:T(8,128)S(1)} copy-done((f32[256,128]{1,0:T(8,128)S(1)}, f32[256,128]{1,0:T(8,128)}, u32[]{:S(2)}) %copy-start.4) | copy-done | bytes 131096
  6.9 0.0 copy-start.5
  6.9 0.9 %copy-done.5 = f32[256,128]{1,0:T(8,128)S(1)} copy-done((f32[256,128]{1,0:T(8,128)S(1)}, f32[256,128]{1,0:T(8,128)}, u32[]{:S(2)}) %copy-start.5) | copy-done | bytes 131096
  7.8 0.0 copy-start.6
  7.8 0.9 %copy-done.6 = bf16[256,256]{1,0:T(8,128)(2,1)S(1)} copy-done((bf16[256,256]{1,0:T(8,128)(2,1)S(1)}, bf16[256,256]{1,0:T(8,128)(2,1)}, u32[]{:S(2)}) %copy-start.6) | copy-done | bytes 131096
  8.7 0.0 copy-start.7
  8.7 0.9 %copy-done.7 = bf16[256,256]{1,0:T(8,128)(2,1)S(1)} copy-done((bf16[256,256]{1,0:T(8,128)(2,1)S(1)}, bf16[256,256]{1,0:T(8,128)(2,1)}, u32[]{:S(2)}) %copy-start.7) | copy-done | bytes 131096
  9.6 0.0 copy-start.8
  9.6 0.8 %copy-done.8 = bf16[1,128,256]{2,1,0:T(8,128)(2,1)S(1)} copy-done((bf16[1,128,256]{2,1,0:T(8,128)(2,1)S(1)}, bf16[1,128,256]{2,1,0:T(8,128)(2,1)}, u32[]{:S(2)}) %copy-start.8) | copy-done | bytes 65560
  10.4 0.0 copy-start.9
  10.4 0.8 %copy-done.9 = bf16[1,128,256]{2,1,0:T(8,128)(2,1)S(1)} copy-done((bf16[1,128,256]{2,1,0:T(8,128)(2,1)S(1)}, bf16[1,128,256]{2,1,0:T(8,128)(2,1)}, u32[]{:S(2)}) %copy-start.9) | copy-done | bytes 65560
  11.3 0.0 copy-start.10
  11.3 0.7 %copy-done.10 = f32[3,256]{1,0:T(4,128)S(1)} copy-done((f32[3,256]{1,0:T(4,128)S(1)}, f32[3,256]{1,0:T(4,128)}, u32[]{:S(2)}) %copy-start.10) | copy-done | bytes 3096
  12.0 0.0 copy-start.11
  12.0 0.7 %copy-done.11 = f32[256]{0:T(256)S(1)} copy-done((f32[256]{0:T(256)S(1)}, f32[256]{0:T(256)}, u32[]{:S(2)}) %copy-start.11) | copy-done | bytes 1048
  12.6 33.9 %shard_map.148 = (f32[128,256]{1,0:T(8,128)S(1)}, f32[128,256]{1,0:T(8,128)S(1)}, f32[128,256]{1,0:T(8,128)S(1)}) custom-call(s32[1]{0:T(128)S(6)} %copy.19.ids_ref, bf16[128,256]{1,0:T(8,128)(2,1)S(1)} %bitcast.9, bf16[128,256]{1,0:T(8,128)(2,1)S(1)} %bitcast.10, f32[128,256]{1,0:T(8,128)S(1)} %copy-done.3, f32[3,256]{1,0:T(4,128)S(1)} %copy-done.10, ...), custom_call_target="tpu_custom_call" | custom-call | tf_op jit(solution)/shard_map/pallas_call | solution.py:338
  46.5 0.7 %copy.20 = f32[1,128,256]{2,1,0:T(8,128)} copy(f32[1,128,256]{2,1,0:T(8,128)S(1)} %bitcast.8) | data formatting | bytes 262144
  47.2 0.7 %copy.21 = f32[1,128,256]{2,1,0:T(8,128)} copy(f32[1,128,256]{2,1,0:T(8,128)S(1)} %bitcast.7) | data formatting | bytes 262144
  47.8 0.7 %copy.22 = f32[128,256]{1,0:T(8,128)} copy(f32[128,256]{1,0:T(8,128)S(1)} %get-tuple-element.14) | data formatting | bytes 262144
Async XLA Ops:
  1.3 1.9 %copy-start = (bf16[6112,256]{1,0:T(8,128)(2,1)S(1)}, bf16[6112,256]{1,0:T(8,128)(2,1)}, u32[]{:S(2)}) copy-start(bf16[6112,256]{1,0:T(8,128)(2,1)} %param.15) | copy-start | bytes 9388036
  3.2 0.9 %copy-start.1 = (bf16[512,256]{1,0:T(8,128)(2,1)S(1)}, bf16[512,256]{1,0:T(8,128)(2,1)}, u32[]{:S(2)}) copy-start(bf16[512,256]{1,0:T(8,128)(2,1)} %constant.13.clone.ll_hbm) | copy-start | bytes 786436
  4.1 0.9 %copy-start.2 = (bf16[512,256]{1,0:T(8,128)(2,1)S(1)}, bf16[512,256]{1,0:T(8,128)(2,1)}, u32[]{:S(2)}) copy-start(bf16[512,256]{1,0:T(8,128)(2,1)} %constant.12.clone.lh_hbm) | copy-start | bytes 786436
  5.1 0.9 %copy-start.3 = (f32[128,256]{1,0:T(8,128)S(1)}, f32[128,256]{1,0:T(8,128)}, u32[]{:S(2)}) copy-start(f32[128,256]{1,0:T(8,128)} %filt_ref.1) | copy-start | bytes 393220
  6.0 0.9 %copy-start.4 = (f32[256,128]{1,0:T(8,128)S(1)}, f32[256,128]{1,0:T(8,128)}, u32[]{:S(2)}) copy-start(f32[256,128]{1,0:T(8,128)} %constant.17.clone.ts_hbm) | copy-start | bytes 393220
  6.9 0.9 %copy-start.5 = (f32[256,128]{1,0:T(8,128)S(1)}, f32[256,128]{1,0:T(8,128)}, u32[]{:S(2)}) copy-start(f32[256,128]{1,0:T(8,128)} %constant.16.clone.tc_hbm) | copy-start | bytes 393220
  7.8 0.9 %copy-start.6 = (bf16[256,256]{1,0:T(8,128)(2,1)S(1)}, bf16[256,256]{1,0:T(8,128)(2,1)}, u32[]{:S(2)}) copy-start(bf16[256,256]{1,0:T(8,128)(2,1)} %constant.15.clone.rl_hbm) | copy-start | bytes 393220
  8.7 0.9 %copy-start.7 = (bf16[256,256]{1,0:T(8,128)(2,1)S(1)}, bf16[256,256]{1,0:T(8,128)(2,1)}, u32[]{:S(2)}) copy-start(bf16[256,256]{1,0:T(8,128)(2,1)} %constant.14.clone.rh_hbm) | copy-start | bytes 393220
  9.6 0.8 %copy-start.8 = (bf16[1,128,256]{2,1,0:T(8,128)(2,1)S(1)}, bf16[1,128,256]{2,1,0:T(8,128)(2,1)}, u32[]{:S(2)}) copy-start(bf16[1,128,256]{2,1,0:T(8,128)(2,1)} %param.13) | copy-start | bytes 196612
  10.4 0.8 %copy-start.9 = (bf16[1,128,256]{2,1,0:T(8,128)(2,1)S(1)}, bf16[1,128,256]{2,1,0:T(8,128)(2,1)}, u32[]{:S(2)}) copy-start(bf16[1,128,256]{2,1,0:T(8,128)(2,1)} %param.19) | copy-start | bytes 196612
  11.3 0.7 %copy-start.10 = (f32[3,256]{1,0:T(4,128)S(1)}, f32[3,256]{1,0:T(4,128)}, u32[]{:S(2)}) copy-start(f32[3,256]{1,0:T(4,128)} %taps_ref.1) | copy-start | bytes 9220
  12.0 0.7 %copy-start.11 = (f32[256]{0:T(256)S(1)}, f32[256]{0:T(256)}, u32[]{:S(2)}) copy-start(f32[256]{0:T(256)} %param.17) | copy-start | bytes 3076

commit v2 on v1

v2 whole, which is shorter than its diff:
```python
import functools
import math

import jax
import jax.numpy as jnp
import numpy as np
from jax import lax
from jax.experimental import pallas as pl
from jax.experimental.pallas import tpu as pltpu
from jax.sharding import PartitionSpec as P

MESH = pl.DeviceIdType.MESH
F32 = jnp.float32
BF16 = jnp.bfloat16
PACK = 8
ROWS16 = 16


def make_table(blocks, samples):
    total = blocks * samples
    index = np.arange(blocks)
    angle = 2.0 * math.pi / blocks * (np.outer(index, index) % blocks)
    spread = np.eye(PACK)
    left = np.concatenate([np.kron(np.cos(angle), spread), -np.kron(np.sin(angle), spread)])
    inner = np.arange(samples)
    angle = 2.0 * math.pi / samples * (np.outer(inner, inner) % samples)
    right = np.block([[np.cos(angle), -np.sin(angle)], [np.sin(angle), np.cos(angle)]])
    turn = 2.0 * math.pi / total * np.outer(index, inner)
    turn = np.repeat(turn, PACK, axis=0)
    turn = np.concatenate([np.cos(turn), np.sin(turn)], axis=1)
    wide = max(left.shape[1], right.shape[1])
    parts = [np.pad(part, ((0, 0), (0, wide - part.shape[1]))) for part in (left, right, turn)]
    return np.concatenate(parts).astype(np.float32)


def split(array):
    high = array.astype(BF16)
    return high, (array - high.astype(F32)).astype(BF16)


def dot(a, b):
    return jnp.dot(a, b, preferred_element_type=F32)


def far_first(step, size):
    shift = lax.div(step + 1, 2)
    return lax.rem(size + size // 2 + jnp.where(lax.rem(step, 2) == 1, -shift, shift), size)


def stencil(field, taps):
    lanes = field.shape[2]
    lane = lax.broadcasted_iota(jnp.int32, field.shape, 2)
    edge = jnp.zeros((1,) + field.shape[1:], F32)
    turned = pltpu.roll(field, 1, 2)
    before = jnp.where(lane == 0, jnp.concatenate([edge, turned[:-1]], axis=0), turned)
    turned = pltpu.roll(field, lanes - 1, 2)
    after = jnp.where(lane == lanes - 1, jnp.concatenate([turned[1:], edge], axis=0), turned)
    return taps[0] * before + taps[1] * field + taps[2] * after


def kernel(
    tm_size,
    dp_size,
    ids_hbm,
    wave_hbm,
    cot_hbm,
    filt_hbm,
    taps_hbm,
    gain_hbm,
    speakers_hbm,
    table_hbm,
    recv_c,
    recv_g,
    ids,
    wave_ref,
    cot_ref,
    filt_ref,
    taps_ref,
    gain_ref,
    speakers,
    table,
    lh,
    ll,
    rh,
    rl,
    send_a,
    recv_a,
    send_f,
    recv_f,
    send_c,
    send_r,
    recv_r,
    send_g,
    local_sem,
    send_sem,
    recv_sem,
):
    dp = lax.axis_index("dp")
    tm = lax.axis_index("tm")
    per = tm_size // dp_size
    place = lax.div(tm, dp_size)
    column_at = lax.rem(tm, dp_size)
    samples = wave_ref.shape[0]
    channels = wave_ref.shape[1]
    rows = tm_size * PACK

    barrier = pltpu.get_barrier_semaphore()

    @pl.loop(1, tm_size)
    def _(step):
        pl.semaphore_signal(
            barrier, inc=1, device_id=(dp, lax.rem(tm + step, tm_size)), device_id_type=MESH
        )

    @pl.loop(1, dp_size)
    def _(step):
        pl.semaphore_signal(
            barrier, inc=1, device_id=(lax.rem(dp + step, dp_size), tm), device_id_type=MESH
        )

    pairs = [
        (wave_hbm, wave_ref),
        (cot_hbm, cot_ref),
        (filt_hbm, filt_ref),
        (table_hbm, table),
        (taps_hbm, taps_ref),
        (gain_hbm, gain_ref),
        (ids_hbm, ids),
        (speakers_hbm, speakers),
    ]
    loads = [
        pltpu.make_async_copy(source, target, local_sem.at[slot])
        for slot, (source, target) in enumerate(pairs)
    ]

    def wait_bytes(like, sem):
        pltpu.make_async_copy(like, like, sem).wait()

    def exchange(source, target, which):
        @pl.loop(0, tm_size - 1)
        def _(step):
            far = far_first(lax.div(step, per), dp_size)
            across = far_first(lax.rem(step, per), per)
            peer = lax.rem(place + across, per) * dp_size + lax.rem(column_at + far, dp_size)
            pltpu.make_async_remote_copy(
                src_ref=source.at[peer],
                dst_ref=target.at[tm],
                send_sem=send_sem.at[which],
                recv_sem=recv_sem.at[which],
                device_id=(dp, peer),
                device_id_type=MESH,
            ).start()

    def to_blocks(field):
        return field.reshape(tm_size, PACK, samples)

    for load in loads[:3]:
        load.start()
    loads[0].wait()
    wave_t = to_blocks(wave_ref[...].astype(F32).T)
    loads[1].wait()
    cot_t = to_blocks(cot_ref[...].astype(F32).T)
    send_a[...] = jnp.concatenate([wave_t, cot_t], axis=1).astype(BF16)
    pl.semaphore_wait(barrier, tm_size - 1 + dp_size - 1)
    exchange(send_a, recv_a, 0)
    recv_a[tm] = send_a[tm]

    loads[2].wait()
    send_f[...] = to_blocks(filt_ref[...].T)
    exchange(send_f, recv_f, 1)
    recv_f[tm] = send_f[tm]

    for load in loads[3:]:
        load.start()
    for load in loads[3:]:
        load.wait()
    lh[...], ll[...] = split(table[: 2 * rows, :rows])
    rh[...], rl[...] = split(table[2 * rows : 2 * rows + 2 * samples, : 2 * samples])
    tc = table[2 * rows + 2 * samples :, :samples]
    ts = table[2 * rows + 2 * samples :, samples : 2 * samples]
    lane = lax.broadcasted_iota(jnp.int32, (PACK, channels), 1)
    row = lax.broadcasted_iota(jnp.int32, (PACK, channels), 0)
    mine = lane == tm * PACK + row

    def column(vector):
        return jnp.sum(jnp.where(mine, vector, 0.0), axis=1, keepdims=True)

    speaker = ids[0]
    group = speakers[lax.div(speaker, ROWS16)]
    picked = lax.broadcasted_iota(jnp.int32, (ROWS16, channels), 0) == lax.rem(speaker, ROWS16)
    speaker_row = jnp.sum(jnp.where(picked, group.astype(F32), 0.0), axis=0, keepdims=True)
    scale = column(speaker_row)
    taps = [column(taps_ref[place : place + 1, :]) for place in range(3)]
    gain = column(gain_ref[...])

    def left_mix(field):
        high, low = split(field)
        return dot(lh[...], high) + (dot(ll[...], high) + dot(lh[...], low))

    def right_mix(field):
        high, low = split(field)
        return dot(high, rh[...]) + (dot(high, rl[...]) + dot(low, rh[...]))

    def twiddle(real, imag):
        return real * tc + imag * ts, imag * tc - real * ts

    def forward(fields):
        mixed = left_mix(jnp.concatenate(fields, axis=1))
        turned = []
        for place in range(len(fields)):
            at = slice(place * samples, (place + 1) * samples)
            turned.append(jnp.concatenate(twiddle(mixed[:rows, at], mixed[rows:, at]), axis=1))
        result = right_mix(jnp.concatenate(turned, axis=0))
        return [
            (
                result[place * rows : (place + 1) * rows, :samples],
                result[place * rows : (place + 1) * rows, samples:],
            )
            for place in range(len(fields))
        ]

    wait_bytes(recv_a.at[pl.ds(0, tm_size - 1)], recv_sem.at[0])
    both = recv_a[...].astype(F32)
    value = stencil(both[:, :PACK], taps) * scale
    grad = both[:, PACK:]
    (vr, vi), (gr, gi) = forward([value.reshape(rows, samples), grad.reshape(rows, samples)])

    inverse_scale = 1.0 / (tm_size * samples)
    term_r = (vr * gr + vi * gi) * inverse_scale
    term_i = (vr * gi - vi * gr) * inverse_scale
    inner = right_mix(jnp.concatenate([term_r, -term_i], axis=1))
    inner_r, inner_i = twiddle(inner[:, :samples], inner[:, samples:])
    high_r, low_r = split(inner_r)
    high_i, low_i = split(inner_i)
    partial = to_blocks(
        dot(lh[:rows, :], high_r)
        + dot(ll[:rows, :], high_r)
        + dot(lh[:rows, :], low_r)
        - dot(lh[rows:, :], high_i)
        - dot(ll[rows:, :], high_i)
        - dot(lh[rows:, :], low_i)
    )

    for block in range(tm_size):
        line = block // dp_size
        send_r[(block - 2 * line) % dp_size, line] = partial[block]

    @pl.loop(0, dp_size - 1)
    def _(step):
        peer = lax.rem(dp + far_first(step, dp_size), dp_size)
        pltpu.make_async_remote_copy(
            src_ref=send_r.at[peer],
            dst_ref=recv_r.at[dp],
            send_sem=send_sem.at[2],
            recv_sem=recv_sem.at[2],
            device_id=(peer, tm),
            device_id_type=MESH,
        ).start()

    recv_r[dp] = send_r[dp]

    wait_bytes(recv_f.at[pl.ds(0, tm_size - 1)], recv_sem.at[1])
    ((fr, fi),) = forward([recv_f[...].reshape(rows, samples)])
    fr = fr * inverse_scale
    fi = fi * inverse_scale
    pr = vr * fr - vi * fi
    pi = vr * fi + vi * fr
    qr = gr * fr + gi * fi
    qi = gi * fr - gr * fi
    inner = right_mix(jnp.concatenate([pr - qi, -(pi + qr)], axis=1))
    inner = jnp.concatenate(twiddle(inner[:, :samples], inner[:, samples:]), axis=1)
    mixed = left_mix(inner)
    convolved = mixed[:rows, :samples] - mixed[rows:, samples:]
    correlated = -mixed[rows:, :samples] - mixed[:rows, samples:]

    layer = to_blocks(convolved) + gain * value
    middle = (to_blocks(correlated) + gain * grad) * scale
    send_c[...] = jnp.concatenate([layer, stencil(middle, taps[::-1])], axis=1)
    exchange(send_c, recv_c, 3)
    own_c = pltpu.make_async_copy(send_c.at[tm], recv_c.at[tm], local_sem.at[8])
    own_c.start()

    wait_bytes(recv_r.at[pl.ds(0, dp_size - 1)], recv_sem.at[2])
    total = recv_r[0]
    for source in range(1, dp_size):
        total = total + recv_r[source]
    send_g[...] = total
    own = lax.rem(dp + 2 * place, dp_size) == column_at
    own_g = pltpu.make_async_copy(send_g.at[place], recv_g.at[tm], local_sem.at[9])

    @pl.loop(0, tm_size)
    def _(step):
        line = lax.rem(place + far_first(lax.rem(step, per), per), per)
        peer_dp = lax.rem(dp + far_first(lax.div(step, per), dp_size), dp_size)
        peer_tm = line * dp_size + lax.rem(dp + 2 * line, dp_size)

        @pl.when(jnp.logical_not((peer_dp == dp) & (peer_tm == tm)))
        def _():
            pltpu.make_async_remote_copy(
                src_ref=send_g.at[line],
                dst_ref=recv_g.at[tm],
                send_sem=send_sem.at[4],
                recv_sem=recv_sem.at[4],
                device_id=(peer_dp, peer_tm),
                device_id_type=MESH,
            ).start()

    wait_bytes(send_a.at[pl.ds(0, tm_size - 1)], send_sem.at[0])
    wait_bytes(send_f.at[pl.ds(0, tm_size - 1)], send_sem.at[1])
    wait_bytes(send_r.at[pl.ds(0, dp_size - 1)], send_sem.at[2])
    wait_bytes(send_c.at[pl.ds(0, tm_size - 1)], send_sem.at[3])
    own_c.wait()
    wait_bytes(recv_c.at[pl.ds(0, tm_size - 1)], recv_sem.at[3])

    @pl.when(own)
    def _():
        own_g.start()
        own_g.wait()
        wait_bytes(recv_g.at[pl.ds(0, tm_size - 1)], send_sem.at[4])
        wait_bytes(recv_g.at[pl.ds(0, tm_size - 1)], recv_sem.at[4])

    @pl.when(jnp.logical_not(own))
    def _():
        wait_bytes(recv_g, send_sem.at[4])
        wait_bytes(recv_g, recv_sem.at[4])


def turn_back(main_hbm, third_hbm, layer_hbm, gradw_hbm, fgrad_hbm, raw, turned, load_sem, store_sem):
    channels, samples = turned.shape[2], turned.shape[1]
    sources = [main_hbm.at[:, :PACK, :], main_hbm.at[:, PACK:, :], third_hbm]
    targets = [layer_hbm, gradw_hbm, fgrad_hbm]
    loads = [
        pltpu.make_async_copy(sources[place], raw.at[place], load_sem.at[place])
        for place in range(3)
    ]
    stores = [
        pltpu.make_async_copy(turned.at[place], targets[place], store_sem.at[place])
        for place in range(3)
    ]
    for load in loads:
        load.start()
    for place in range(3):
        loads[place].wait()
        turned[place] = raw[place].reshape(channels, samples).T
        stores[place].start()
    for store in stores:
        store.wait()


def local(waveform, speaker_ids, speaker_table, stencil_taps, skip_gain, filters, cotangent):
    tm_size, dp_size = lax.axis_size("tm"), lax.axis_size("dp")
    samples, channels = filters.shape
    per = tm_size // dp_size
    rows = tm_size * PACK
    table = make_table(tm_size, samples)
    anywhere = pl.BlockSpec(memory_space=pl.ANY)
    block = jax.ShapeDtypeStruct((samples, channels), F32)
    main, third = pl.pallas_call(
        functools.partial(kernel, tm_size, dp_size),
        out_shape=[
            jax.ShapeDtypeStruct((tm_size, 2 * PACK, samples), F32),
            jax.ShapeDtypeStruct((tm_size, PACK, samples), F32),
        ],
        in_specs=[anywhere] * 8,
        out_specs=[anywhere] * 2,
        scratch_shapes=[
            pltpu.SMEM((1,), jnp.int32),
            pltpu.VMEM((samples, channels), BF16),
            pltpu.VMEM((samples, channels), BF16),
            pltpu.VMEM((samples, channels), F32),
            pltpu.VMEM(stencil_taps.shape, F32),
            pltpu.VMEM((1, channels), F32),
            pltpu.VMEM((speaker_table.shape[0] // ROWS16, ROWS16, channels), BF16),
            pltpu.VMEM(table.shape, F32),
            pltpu.VMEM((2 * rows, rows), BF16),
            pltpu.VMEM((2 * rows, rows), BF16),
            pltpu.VMEM((2 * samples, 2 * samples), BF16),
            pltpu.VMEM((2 * samples, 2 * samples), BF16),
            pltpu.VMEM((tm_size, 2 * PACK, samples), BF16),
            pltpu.VMEM((tm_size, 2 * PACK, samples), BF16),
            pltpu.VMEM((tm_size, PACK, samples), F32),
            pltpu.VMEM((tm_size, PACK, samples), F32),
            pltpu.VMEM((tm_size, 2 * PACK, samples), F32),
            pltpu.VMEM((dp_size, per, PACK, samples), F32),
            pltpu.VMEM((dp_size, per, PACK, samples), F32),
            pltpu.VMEM((per, PACK, samples), F32),
            pltpu.SemaphoreType.DMA((10,)),
            pltpu.SemaphoreType.DMA((5,)),
            pltpu.SemaphoreType.DMA((5,)),
        ],
        compiler_params=pltpu.CompilerParams(
            collective_id=0, has_side_effects=True, vmem_limit_bytes=62 * 1024 * 1024
        ),
    )(
        speaker_ids,
        waveform[0],
        cotangent[0],
        filters,
        stencil_taps,
        skip_gain[None],
        speaker_table.reshape(-1, ROWS16, channels),
        jnp.asarray(table),
    )
    layer_out, grad_waveform, filter_grad = pl.pallas_call(
        turn_back,
        out_shape=[block, block, block],
        in_specs=[anywhere] * 2,
        out_specs=[anywhere] * 3,
        scratch_shapes=[
            pltpu.VMEM((3, tm_size, PACK, samples), F32),
            pltpu.VMEM((3, samples, channels), F32),
            pltpu.SemaphoreType.DMA((3,)),
            pltpu.SemaphoreType.DMA((3,)),
        ],
        compiler_params=pltpu.CompilerParams(vmem_limit_bytes=62 * 1024 * 1024),
    )(main, third)
    return layer_out[None], grad_waveform[None], filter_grad


def solution(mesh):
    return jax.shard_map(
        local,
        mesh=mesh,
        in_specs=(P("dp", "tm", None), P("dp"), P(), P(), P(), P("tm", None), P("dp", "tm", None)),
        out_specs=(P("dp", "tm", None), P("dp", "tm", None), P("tm", None)),
        check_vma=False,
    )
```

time: 48.9 us -> 38 us (0.78)
  the two profiles are of different devices: /device:TPU:7 before, /device:TPU:1 now
where the time goes in v2:
time: 38 us; the launch traced here: 37.4 us
  Pallas kernels  36.2 us (95%)
  between operations  1.29 us (3%)
    pallas_call x1, Pallas kernels, local(): pl.pallas_call(functools.partial(kernel, tm_size, dp_size), out_shape=[ja...  34.2 us
    pallas_call x1, Pallas kernels, local(): pl.pallas_call(turn_back, out_shape=[block, block, block], in_specs=[anyw...  1.92 us

profile of v2, /device:TPU:1, one launch (start us, length us, event | category | flops | bytes accessed | tf_op | source)
XLA Modules:
  0.0 37.4 jit_solution(17146769912262997429)
XLA Ops:
  1.3 34.2 %shard_map.103 = (f32[32,16,128]{2,1,0:T(8,128)}, f32[32,8,128]{2,1,0:T(8,128)}) custom-call(s32[1]{0:T(128)S(6)} %copy.11.ids_hbm, bf16[128,256]{1,0:T(8,128)(2,1)} %bitcast.7, bf16[128,256]{1,0:T(8,128)(2,1)} %bitcast.8, f32[128,256]{1,0:T(8,128)} %filt_hbm.1, f32[3,256]{1,0:T(4,128)} %taps_hbm.1, f32[1,256]{1,0:T(1,128)} %bitcast.9, ...), custom_call_target="tpu_custom_call" | custom-call | tf_op jit(solution)/shard_map/pallas_call | solution.py:358
  35.5 1.9 %shard_map.104 = (f32[128,256]{1,0:T(8,128)}, f32[128,256]{1,0:T(8,128)}, f32[128,256]{1,0:T(8,128)}) custom-call(f32[32,16,128]{2,1,0:T(8,128)} %get-tuple-element.8.main_hbm, f32[32,8,128]{2,1,0:T(8,128)} %get-tuple-element.9.third_hbm), custom_call_target="tpu_custom_call" | custom-call | tf_op jit(solution)/shard_map/pallas_call | solution.py:404

commit v3 on v2

--- a/solution.py
+++ b/solution.py
@@ -69,7 +69,8 @@
     gain_hbm,
     speakers_hbm,
     table_hbm,
-    recv_c,
+    recv_l,
+    recv_w,
     recv_g,
     ids,
     wave_ref,
@@ -87,13 +88,15 @@
     recv_a,
     send_f,
     recv_f,
-    send_c,
+    send_l,
+    send_w,
     send_r,
     recv_r,
     send_g,
     local_sem,
     send_sem,
     recv_sem,
+    plane_sem,
 ):
     dp = lax.axis_index("dp")
     tm = lax.axis_index("tm")
@@ -106,17 +109,21 @@
 
     barrier = pltpu.get_barrier_semaphore()
 
-    @pl.loop(1, tm_size)
+    def tm_peer(step):
+        far = far_first(lax.div(step, per), dp_size)
+        across = far_first(lax.rem(step, per), per)
+        return lax.rem(place + across, per) * dp_size + lax.rem(column_at + far, dp_size)
+
+    def dp_peer(step):
+        return lax.rem(dp + far_first(step, dp_size), dp_size)
+
+    @pl.loop(0, tm_size - 1)
     def _(step):
-        pl.semaphore_signal(
-            barrier, inc=1, device_id=(dp, lax.rem(tm + step, tm_size)), device_id_type=MESH
-        )
-
-    @pl.loop(1, dp_size)
+        pl.semaphore_signal(barrier, inc=1, device_id=(dp, tm_peer(step)), device_id_type=MESH)
+
+    @pl.loop(0, dp_size - 1)
     def _(step):
-        pl.semaphore_signal(
-            barrier, inc=1, device_id=(lax.rem(dp + step, dp_size), tm), device_id_type=MESH
-        )
+        pl.semaphore_signal(barrier, inc=1, device_id=(dp_peer(step), tm), device_id_type=MESH)
 
     pairs = [
         (wave_hbm, wave_ref),
@@ -139,9 +146,7 @@
     def exchange(source, target, which):
         @pl.loop(0, tm_size - 1)
         def _(step):
-            far = far_first(lax.div(step, per), dp_size)
-            across = far_first(lax.rem(step, per), per)
-            peer = lax.rem(place + across, per) * dp_size + lax.rem(column_at + far, dp_size)
+            peer = tm_peer(step)
             pltpu.make_async_remote_copy(
                 src_ref=source.at[peer],
                 dst_ref=target.at[tm],
@@ -164,6 +169,14 @@
     pl.semaphore_wait(barrier, tm_size - 1 + dp_size - 1)
     exchange(send_a, recv_a, 0)
     recv_a[tm] = send_a[tm]
+
+    adder = lax.div(tm, per)
+
+    @pl.when(adder == dp)
+    def _():
+        @pl.loop(0, dp_size - 1)
+        def _(step):
+            pl.semaphore_signal(plane_sem, inc=1, device_id=(dp_peer(step), tm), device_id_type=MESH)
 
     loads[2].wait()
     send_f[...] = to_blocks(filt_ref[...].T)
@@ -232,7 +245,7 @@
     inner_r, inner_i = twiddle(inner[:, :samples], inner[:, samples:])
     high_r, low_r = split(inner_r)
     high_i, low_i = split(inner_i)
-    partial = to_blocks(
+    send_r[...] = to_blocks(
         dot(lh[:rows, :], high_r)
         + dot(ll[:rows, :], high_r)
         + dot(lh[:rows, :], low_r)
@@ -241,23 +254,33 @@
         - dot(lh[rows:, :], low_i)
     )
 
-    for block in range(tm_size):
-        line = block // dp_size
-        send_r[(block - 2 * line) % dp_size, line] = partial[block]
-
-    @pl.loop(0, dp_size - 1)
-    def _(step):
-        peer = lax.rem(dp + far_first(step, dp_size), dp_size)
+    @pl.when(adder != dp)
+    def _():
+        pl.semaphore_wait(plane_sem, 1)
+
+    slot = dp * per + lax.rem(tm, per)
+
+    def send_partial(block):
         pltpu.make_async_remote_copy(
-            src_ref=send_r.at[peer],
-            dst_ref=recv_r.at[dp],
+            src_ref=send_r.at[block],
+            dst_ref=recv_r.at[slot],
             send_sem=send_sem.at[2],
             recv_sem=recv_sem.at[2],
-            device_id=(peer, tm),
+            device_id=(adder, block),
             device_id_type=MESH,
         ).start()
 
-    recv_r[dp] = send_r[dp]
+    @pl.loop(0, tm_size - 1)
+    def _(step):
+        send_partial(tm_peer(step))
+
+    @pl.when(adder != dp)
+    def _():
+        send_partial(tm)
+
+    @pl.when(adder == dp)
+    def _():
+        recv_r[slot] = send_r[tm]
 
     wait_bytes(recv_f.at[pl.ds(0, tm_size - 1)], recv_sem.at[1])
     ((fr, fi),) = forward([recv_f[...].reshape(rows, samples)])
@@ -273,61 +296,68 @@
     convolved = mixed[:rows, :samples] - mixed[rows:, samples:]
     correlated = -mixed[rows:, :samples] - mixed[:rows, samples:]
 
-    layer = to_blocks(convolved) + gain * value
+    send_l[...] = to_blocks(convolved) + gain * value
+    exchange(send_l, recv_l, 3)
     middle = (to_blocks(correlated) + gain * grad) * scale
-    send_c[...] = jnp.concatenate([layer, stencil(middle, taps[::-1])], axis=1)
-    exchange(send_c, recv_c, 3)
-    own_c = pltpu.make_async_copy(send_c.at[tm], recv_c.at[tm], local_sem.at[8])
-    own_c.start()
-
-    wait_bytes(recv_r.at[pl.ds(0, dp_size - 1)], recv_sem.at[2])
-    total = recv_r[0]
-    for source in range(1, dp_size):
-        total = total + recv_r[source]
-    send_g[...] = total
-    own = lax.rem(dp + 2 * place, dp_size) == column_at
-    own_g = pltpu.make_async_copy(send_g.at[place], recv_g.at[tm], local_sem.at[9])
-
-    @pl.loop(0, tm_size)
+    send_w[...] = stencil(middle, taps[::-1])
+
+    exchange(send_w, recv_w, 5)
+    own_l = pltpu.make_async_copy(send_l.at[tm], recv_l.at[tm], local_sem.at[8])
+    own_w = pltpu.make_async_copy(send_w.at[tm], recv_w.at[tm], local_sem.at[10])
+    own_l.start()
+    own_w.start()
+
+    @pl.when(adder == dp)
+    def _():
+        wait_bytes(recv_r.at[pl.ds(0, tm_size - 1)], recv_sem.at[2])
+
+    @pl.when(adder != dp)
+    def _():
+        wait_bytes(recv_r, recv_sem.at[2])
+
+    send_g[...] = jnp.sum(recv_r[...].reshape(dp_size, per, PACK, samples), axis=0)
+    summed = recv_g.at[pl.ds(dp * per, per)]
+
+    @pl.loop(0, dp_size - 1)
     def _(step):
-        line = lax.rem(place + far_first(lax.rem(step, per), per), per)
-        peer_dp = lax.rem(dp + far_first(lax.div(step, per), dp_size), dp_size)
-        peer_tm = line * dp_size + lax.rem(dp + 2 * line, dp_size)
-
-        @pl.when(jnp.logical_not((peer_dp == dp) & (peer_tm == tm)))
-        def _():
-            pltpu.make_async_remote_copy(
-                src_ref=send_g.at[line],
-                dst_ref=recv_g.at[tm],
-                send_sem=send_sem.at[4],
-                recv_sem=recv_sem.at[4],
-                device_id=(peer_dp, peer_tm),
-                device_id_type=MESH,
-            ).start()
-
+        pltpu.make_async_remote_copy(
+            src_ref=send_g,
+            dst_ref=summed,
+            send_sem=send_sem.at[4],
+            recv_sem=recv_sem.at[4],
+            device_id=(dp_peer(step), tm),
+            device_id_type=MESH,
+        ).start()
+
+    own_g = pltpu.make_async_copy(send_g, summed, local_sem.at[9])
+    own_g.start()
     wait_bytes(send_a.at[pl.ds(0, tm_size - 1)], send_sem.at[0])
     wait_bytes(send_f.at[pl.ds(0, tm_size - 1)], send_sem.at[1])
-    wait_bytes(send_r.at[pl.ds(0, dp_size - 1)], send_sem.at[2])
-    wait_bytes(send_c.at[pl.ds(0, tm_size - 1)], send_sem.at[3])
-    own_c.wait()
-    wait_bytes(recv_c.at[pl.ds(0, tm_size - 1)], recv_sem.at[3])
-
-    @pl.when(own)
-    def _():
-        own_g.start()
-        own_g.wait()
-        wait_bytes(recv_g.at[pl.ds(0, tm_size - 1)], send_sem.at[4])
-        wait_bytes(recv_g.at[pl.ds(0, tm_size - 1)], recv_sem.at[4])
-
-    @pl.when(jnp.logical_not(own))
-    def _():
-        wait_bytes(recv_g, send_sem.at[4])
-        wait_bytes(recv_g, recv_sem.at[4])
-
-
-def turn_back(main_hbm, third_hbm, layer_hbm, gradw_hbm, fgrad_hbm, raw, turned, load_sem, store_sem):
+    wait_bytes(send_l.at[pl.ds(0, tm_size - 1)], send_sem.at[3])
+    wait_bytes(send_w.at[pl.ds(0, tm_size - 1)], send_sem.at[5])
+
+    @pl.when(adder == dp)
+    def _():
+        wait_bytes(send_r.at[pl.ds(0, tm_size - 1)], send_sem.at[2])
+
+    @pl.when(adder != dp)
+    def _():
+        wait_bytes(send_r, send_sem.at[2])
+
+    wait_bytes(recv_r.at[pl.ds(0, tm_size - per)], send_sem.at[4])
+    own_l.wait()
+    own_w.wait()
+    own_g.wait()
+    wait_bytes(recv_l.at[pl.ds(0, tm_size - 1)], recv_sem.at[3])
+    wait_bytes(recv_w.at[pl.ds(0, tm_size - 1)], recv_sem.at[5])
+    wait_bytes(recv_g.at[pl.ds(0, tm_size - per)], recv_sem.at[4])
+
+
+def turn_back(
+    raw_layer, raw_gradw, raw_fgrad, layer_hbm, gradw_hbm, fgrad_hbm, raw, turned, load_sem, store_sem
+):
     channels, samples = turned.shape[2], turned.shape[1]
-    sources = [main_hbm.at[:, :PACK, :], main_hbm.at[:, PACK:, :], third_hbm]
+    sources = [raw_layer, raw_gradw, raw_fgrad]
     targets = [layer_hbm, gradw_hbm, fgrad_hbm]
     loads = [
         pltpu.make_async_copy(sources[place], raw.at[place], load_sem.at[place])
@@ -355,14 +385,12 @@
     table = make_table(tm_size, samples)
     anywhere = pl.BlockSpec(memory_space=pl.ANY)
     block = jax.ShapeDtypeStruct((samples, channels), F32)
-    main, third = pl.pallas_call(
+    pieces = jax.ShapeDtypeStruct((tm_size, PACK, samples), F32)
+    received = pl.pallas_call(
         functools.partial(kernel, tm_size, dp_size),
-        out_shape=[
-            jax.ShapeDtypeStruct((tm_size, 2 * PACK, samples), F32),
-            jax.ShapeDtypeStruct((tm_size, PACK, samples), F32),
-        ],
+        out_shape=[pieces] * 3,
         in_specs=[anywhere] * 8,
-        out_specs=[anywhere] * 2,
+        out_specs=[anywhere] * 3,
         scratch_shapes=[
             pltpu.SMEM((1,), jnp.int32),
             pltpu.VMEM((samples, channels), BF16),
@@ -380,13 +408,15 @@
             pltpu.VMEM((tm_size, 2 * PACK, samples), BF16),
             pltpu.VMEM((tm_size, PACK, samples), F32),
             pltpu.VMEM((tm_size, PACK, samples), F32),
-            pltpu.VMEM((tm_size, 2 * PACK, samples), F32),
-            pltpu.VMEM((dp_size, per, PACK, samples), F32),
-            pltpu.VMEM((dp_size, per, PACK, samples), F32),
+            pltpu.VMEM((tm_size, PACK, samples), F32),
+            pltpu.VMEM((tm_size, PACK, samples), F32),
+            pltpu.VMEM((tm_size, PACK, samples), F32),
+            pltpu.VMEM((tm_size, PACK, samples), F32),
             pltpu.VMEM((per, PACK, samples), F32),
-            pltpu.SemaphoreType.DMA((10,)),
-            pltpu.SemaphoreType.DMA((5,)),
-            pltpu.SemaphoreType.DMA((5,)),
+            pltpu.SemaphoreType.DMA((11,)),
+            pltpu.SemaphoreType.DMA((6,)),
+            pltpu.SemaphoreType.DMA((6,)),
+            pltpu.SemaphoreType.REGULAR,
         ],
         compiler_params=pltpu.CompilerParams(
             collective_id=0, has_side_effects=True, vmem_limit_bytes=62 * 1024 * 1024
@@ -404,7 +434,7 @@
     layer_out, grad_waveform, filter_grad = pl.pallas_call(
         turn_back,
         out_shape=[block, block, block],
-        in_specs=[anywhere] * 2,
+        in_specs=[anywhere] * 3,
         out_specs=[anywhere] * 3,
         scratch_shapes=[
             pltpu.VMEM((3, tm_size, PACK, samples), F32),
@@ -413,7 +443,7 @@
             pltpu.SemaphoreType.DMA((3,)),
         ],
         compiler_params=pltpu.CompilerParams(vmem_limit_bytes=62 * 1024 * 1024),
-    )(main, third)
+    )(*received)
     return layer_out[None], grad_waveform[None], filter_grad
 
 

time: 38 us -> 35.5 us (0.934); the launches traced: 37.4 us -> 35.4 us
  Pallas kernels: 36.2 us -> 34.1 us
    pallas_call x1, Pallas kernels: 34.2 us -> 32.2 us  [local(): pl.pallas_call(functools.partial(kernel, tm_size, dp_size), out_shape=[pi...]
where the time goes in v3:
time: 35.5 us; the launch traced here: 35.4 us
  Pallas kernels  34.1 us (96%)
  between operations  1.29 us (4%)
    pallas_call x1, Pallas kernels, local(): pl.pallas_call(functools.partial(kernel, tm_size, dp_size), out_shape=[pi...  32.2 us
    pallas_call x1, Pallas kernels, local(): pl.pallas_call(turn_back, out_shape=[block, block, block], in_specs=[anyw...  1.92 us

profile of v3, /device:TPU:1, one launch (start us, length us, event | category | flops | bytes accessed | tf_op | source)
XLA Modules:
  0.0 35.4 jit_solution(10842795723064095485)
XLA Ops:
  1.3 32.2 %shard_map.103 = (f32[32,8,128]{2,1,0:T(8,128)}, f32[32,8,128]{2,1,0:T(8,128)}, f32[32,8,128]{2,1,0:T(8,128)}) custom-call(s32[1]{0:T(128)S(6)} %copy.11.ids_hbm, bf16[128,256]{1,0:T(8,128)(2,1)} %bitcast.7, bf16[128,256]{1,0:T(8,128)(2,1)} %bitcast.8, f32[128,256]{1,0:T(8,128)} %filt_hbm.1, f32[3,256]{1,0:T(4,128)} %taps_hbm.1, f32[1,256]{1,0:T(1,128)} %bitcast.9, ...), custom_call_target="tpu_custom_call" | custom-call | tf_op jit(solution)/shard_map/pallas_call | solution.py:389
  33.5 1.9 %shard_map.104 = (f32[128,256]{1,0:T(8,128)}, f32[128,256]{1,0:T(8,128)}, f32[128,256]{1,0:T(8,128)}) custom-call(f32[32,8,128]{2,1,0:T(8,128)} %get-tuple-element.9.raw_layer, f32[32,8,128]{2,1,0:T(8,128)} %get-tuple-element.10.raw_gradw, f32[32,8,128]{2,1,0:T(8,128)} %get-tuple-element.11.raw_fgrad), custom_call_target="tpu_custom_call" | custom-call | tf_op jit(solution)/shard_map/pallas_call | solution.py:434

commit v4 on v3

--- a/solution.py
+++ b/solution.py
@@ -18,18 +18,21 @@
 
 def make_table(blocks, samples):
     total = blocks * samples
-    index = np.arange(blocks)
-    angle = 2.0 * math.pi / blocks * (np.outer(index, index) % blocks)
     spread = np.eye(PACK)
-    left = np.concatenate([np.kron(np.cos(angle), spread), -np.kron(np.sin(angle), spread)])
+    block = np.arange(blocks)
+    low = np.arange(blocks // 2 + 1)
+    angle = 2.0 * math.pi / blocks * (np.outer(low, block) % blocks)
+    forward = np.concatenate([np.cos(angle), -np.sin(angle)[1:-1]])
+    weight = np.where((low == 0) | (low == blocks // 2), 1.0, 2.0)[:, None] / total
+    backward = np.concatenate([weight * np.cos(angle), (weight * np.sin(angle))[1:-1]]).T
     inner = np.arange(samples)
     angle = 2.0 * math.pi / samples * (np.outer(inner, inner) % samples)
     right = np.block([[np.cos(angle), -np.sin(angle)], [np.sin(angle), np.cos(angle)]])
-    turn = 2.0 * math.pi / total * np.outer(index, inner)
-    turn = np.repeat(turn, PACK, axis=0)
+    turn = np.repeat(2.0 * math.pi / total * np.outer(low, inner), PACK, axis=0)
     turn = np.concatenate([np.cos(turn), np.sin(turn)], axis=1)
-    wide = max(left.shape[1], right.shape[1])
-    parts = [np.pad(part, ((0, 0), (0, wide - part.shape[1]))) for part in (left, right, turn)]
+    parts = [np.kron(forward, spread), np.kron(backward, spread), right, turn]
+    wide = max(part.shape[1] for part in parts)
+    parts = [np.pad(part, ((0, 0), (0, wide - part.shape[1]))) for part in parts]
     return np.concatenate(parts).astype(np.float32)
 
 
@@ -40,6 +43,72 @@
 
 def dot(a, b):
     return jnp.dot(a, b, preferred_element_type=F32)
+
+
+def quantize(field):
+    peak = jnp.max(jnp.abs(field), axis=2, keepdims=True)
+    power = jnp.floor(4.0 * jnp.log2(32000.0 / jnp.maximum(peak, 1e-30)))
+    return jnp.round(field * jnp.exp2(0.25 * power)).astype(jnp.int32), power + 512.0
+
+
+def step_size(power):
+    return jnp.exp2(0.25 * (512.0 - power))
+
+
+def diagonal(blocks, lanes):
+    shape = (blocks, PACK, lanes)
+    return lax.broadcasted_iota(jnp.int32, shape, 1) == lax.broadcasted_iota(jnp.int32, shape, 2)
+
+
+def lay_out(power, lanes):
+    spread = jnp.where(diagonal(power.shape[0], lanes), power, 0.0)
+    return jnp.sum(spread, axis=1, keepdims=True).astype(jnp.int32)
+
+
+def stand_up(row):
+    spread = jnp.where(diagonal(row.shape[0], row.shape[2]), row.astype(F32), 0.0)
+    return jnp.sum(spread, axis=2, keepdims=True)
+
+
+def pair(high, low):
+    return (high << 16) | (low & 0xFFFF)
+
+
+def first_of(word):
+    return (word >> 16).astype(F32)
+
+
+def second_of(word):
+    return ((word << 16) >> 16).astype(F32)
+
+
+def encode_one(field, target):
+    steps, power = quantize(field)
+    half = PACK // 2
+    target[:, :half] = pair(steps, pltpu.roll(steps, half, 1))[:, :half]
+    target[:, half:] = lay_out(power, field.shape[2])
+
+
+def decode_one(source):
+    half = PACK // 2
+    words = source[:, :half]
+    power = stand_up(source[:, half:])
+    return jnp.concatenate([first_of(words), second_of(words)], axis=1) * step_size(power)
+
+
+def encode_two(first, second, target):
+    first_steps, first_power = quantize(first)
+    second_steps, second_power = quantize(second)
+    target[:, :PACK] = pair(first_steps, second_steps)
+    target[:, PACK:] = lay_out(first_power + 1024.0 * second_power, first.shape[2])
+
+
+def decode_two(source):
+    words = source[:, :PACK]
+    powers = stand_up(source[:, PACK:]).astype(jnp.int32)
+    first_power = (powers & 1023).astype(F32)
+    second_power = (powers >> 10).astype(F32)
+    return first_of(words) * step_size(first_power), second_of(words) * step_size(second_power)
 
 
 def far_first(step, size):
@@ -69,8 +138,7 @@
     gain_hbm,
     speakers_hbm,
     table_hbm,
-    recv_l,
-    recv_w,
+    recv_c,
     recv_g,
     ids,
     wave_ref,
@@ -82,14 +150,15 @@
     table,
     lh,
     ll,
+    bh,
+    bl,
     rh,
     rl,
     send_a,
     recv_a,
     send_f,
     recv_f,
-    send_l,
-    send_w,
+    send_c,
     send_r,
     recv_r,
     send_g,
@@ -179,7 +248,7 @@
             pl.semaphore_signal(plane_sem, inc=1, device_id=(dp_peer(step), tm), device_id_type=MESH)
 
     loads[2].wait()
-    send_f[...] = to_blocks(filt_ref[...].T)
+    encode_one(to_blocks(filt_ref[...].T), send_f)
     exchange(send_f, recv_f, 1)
     recv_f[tm] = send_f[tm]
 
@@ -187,7 +256,8 @@
         load.start()
     for load in loads[3:]:
         load.wait()
-    lh[...], ll[...] = split(table[: 2 * rows, :rows])
+    lh[...], ll[...] = split(table[:rows, :rows])
+    bh[...], bl[...] = split(table[rows : 2 * rows, :rows])
     rh[...], rl[...] = split(table[2 * rows : 2 * rows + 2 * samples, : 2 * samples])
     tc = table[2 * rows + 2 * samples :, :samples]
     ts = table[2 * rows + 2 * samples :, samples : 2 * samples]
@@ -206,10 +276,6 @@
     taps = [column(taps_ref[place : place + 1, :]) for place in range(3)]
     gain = column(gain_ref[...])
 
-    def left_mix(field):
-        high, low = split(field)
-        return dot(lh[...], high) + (dot(ll[...], high) + dot(lh[...], low))
-
     def right_mix(field):
         high, low = split(field)
         return dot(high, rh[...]) + (dot(high, rl[...]) + dot(low, rh[...]))
@@ -217,42 +283,42 @@
     def twiddle(real, imag):
         return real * tc + imag * ts, imag * tc - real * ts
 
-    def forward(fields):
-        mixed = left_mix(jnp.concatenate(fields, axis=1))
+    half_rows = (tm_size // 2 + 1) * PACK
+
+    def forward(mixed):
+        count = mixed.shape[1] // samples
+        blank = jnp.zeros((PACK, samples), F32)
         turned = []
-        for place in range(len(fields)):
-            at = slice(place * samples, (place + 1) * samples)
-            turned.append(jnp.concatenate(twiddle(mixed[:rows, at], mixed[rows:, at]), axis=1))
+        for field in range(count):
+            part = mixed[:, field * samples : (field + 1) * samples]
+            imag = jnp.concatenate([blank, part[half_rows:], blank], axis=0)
+            turned.append(jnp.concatenate(twiddle(part[:half_rows], imag), axis=1))
         result = right_mix(jnp.concatenate(turned, axis=0))
-        return [
-            (
-                result[place * rows : (place + 1) * rows, :samples],
-                result[place * rows : (place + 1) * rows, samples:],
-            )
-            for place in range(len(fields))
-        ]
+        parts = [result[field * half_rows : (field + 1) * half_rows] for field in range(count)]
+        return [(part[:, :samples], part[:, samples:]) for part in parts]
+
+    def backward(spectra):
+        packed = [jnp.concatenate([real, -imag], axis=1) for real, imag in spectra]
+        inner = right_mix(jnp.concatenate(packed, axis=0))
+        turned = []
+        for field in range(len(spectra)):
+            part = inner[field * half_rows : (field + 1) * half_rows]
+            real, imag = twiddle(part[:, :samples], part[:, samples:])
+            turned.append(jnp.concatenate([real, imag[PACK:-PACK]], axis=0))
+        high, low = split(jnp.concatenate(turned, axis=1))
+        return dot(bh[...], high) + (dot(bl[...], high) + dot(bh[...], low))
 
     wait_bytes(recv_a.at[pl.ds(0, tm_size - 1)], recv_sem.at[0])
     both = recv_a[...].astype(F32)
     value = stencil(both[:, :PACK], taps) * scale
     grad = both[:, PACK:]
-    (vr, vi), (gr, gi) = forward([value.reshape(rows, samples), grad.reshape(rows, samples)])
-
-    inverse_scale = 1.0 / (tm_size * samples)
-    term_r = (vr * gr + vi * gi) * inverse_scale
-    term_i = (vr * gi - vi * gr) * inverse_scale
-    inner = right_mix(jnp.concatenate([term_r, -term_i], axis=1))
-    inner_r, inner_i = twiddle(inner[:, :samples], inner[:, samples:])
-    high_r, low_r = split(inner_r)
-    high_i, low_i = split(inner_i)
-    send_r[...] = to_blocks(
-        dot(lh[:rows, :], high_r)
-        + dot(ll[:rows, :], high_r)
-        + dot(lh[:rows, :], low_r)
-        - dot(lh[rows:, :], high_i)
-        - dot(ll[rows:, :], high_i)
-        - dot(lh[rows:, :], low_i)
-    )
+    value_high, value_low = split(value.reshape(rows, samples))
+    high = jnp.concatenate([value_high, grad.reshape(rows, samples).astype(BF16)], axis=1)
+    mixed = dot(lh[...], high) + dot(ll[...], high)
+    mixed_value = mixed[:, :samples] + dot(lh[...], value_low)
+    mixed = jnp.concatenate([mixed_value, mixed[:, samples:]], axis=1)
+    (vr, vi), (gr, gi) = forward(mixed)
+    encode_one(to_blocks(backward([(vr * gr + vi * gi, vr * gi - vi * gr)])), send_r)
 
     @pl.when(adder != dp)
     def _():
@@ -283,29 +349,21 @@
         recv_r[slot] = send_r[tm]
 
     wait_bytes(recv_f.at[pl.ds(0, tm_size - 1)], recv_sem.at[1])
-    ((fr, fi),) = forward([recv_f[...].reshape(rows, samples)])
-    fr = fr * inverse_scale
-    fi = fi * inverse_scale
-    pr = vr * fr - vi * fi
-    pi = vr * fi + vi * fr
-    qr = gr * fr + gi * fi
-    qi = gi * fr - gr * fi
-    inner = right_mix(jnp.concatenate([pr - qi, -(pi + qr)], axis=1))
-    inner = jnp.concatenate(twiddle(inner[:, :samples], inner[:, samples:]), axis=1)
-    mixed = left_mix(inner)
-    convolved = mixed[:rows, :samples] - mixed[rows:, samples:]
-    correlated = -mixed[rows:, :samples] - mixed[:rows, samples:]
-
-    send_l[...] = to_blocks(convolved) + gain * value
-    exchange(send_l, recv_l, 3)
+    high, low = split(decode_one(recv_f).reshape(rows, samples))
+    ((fr, fi),) = forward(dot(lh[...], high) + (dot(ll[...], high) + dot(lh[...], low)))
+    results = backward(
+        [
+            (vr * fr - vi * fi, vr * fi + vi * fr),
+            (gr * fr + gi * fi, gi * fr - gr * fi),
+        ]
+    )
+    convolved, correlated = results[:, :samples], results[:, samples:]
+    layer = to_blocks(convolved) + gain * value
     middle = (to_blocks(correlated) + gain * grad) * scale
-    send_w[...] = stencil(middle, taps[::-1])
-
-    exchange(send_w, recv_w, 5)
-    own_l = pltpu.make_async_copy(send_l.at[tm], recv_l.at[tm], local_sem.at[8])
-    own_w = pltpu.make_async_copy(send_w.at[tm], recv_w.at[tm], local_sem.at[10])
-    own_l.start()
-    own_w.start()
+    encode_two(layer, stencil(middle, taps[::-1]), send_c)
+    exchange(send_c, recv_c, 3)
+    own_c = pltpu.make_async_copy(send_c.at[tm], recv_c.at[tm], local_sem.at[8])
+    own_c.start()
 
     @pl.when(adder == dp)
     def _():
@@ -315,7 +373,7 @@
     def _():
         wait_bytes(recv_r, recv_sem.at[2])
 
-    send_g[...] = jnp.sum(recv_r[...].reshape(dp_size, per, PACK, samples), axis=0)
+    send_g[...] = jnp.sum(decode_one(recv_r).reshape(dp_size, per, PACK, samples), axis=0)
     summed = recv_g.at[pl.ds(dp * per, per)]
 
     @pl.loop(0, dp_size - 1)
@@ -333,8 +391,7 @@
     own_g.start()
     wait_bytes(send_a.at[pl.ds(0, tm_size - 1)], send_sem.at[0])
     wait_bytes(send_f.at[pl.ds(0, tm_size - 1)], send_sem.at[1])
-    wait_bytes(send_l.at[pl.ds(0, tm_size - 1)], send_sem.at[3])
-    wait_bytes(send_w.at[pl.ds(0, tm_size - 1)], send_sem.at[5])
+    wait_bytes(send_c.at[pl.ds(0, tm_size - 1)], send_sem.at[3])
 
     @pl.when(adder == dp)
     def _():
@@ -344,35 +401,39 @@
     def _():
         wait_bytes(send_r, send_sem.at[2])
 
-    wait_bytes(recv_r.at[pl.ds(0, tm_size - per)], send_sem.at[4])
-    own_l.wait()
-    own_w.wait()
+    wait_bytes(recv_g.at[pl.ds(0, tm_size - per)], send_sem.at[4])
+    own_c.wait()
     own_g.wait()
-    wait_bytes(recv_l.at[pl.ds(0, tm_size - 1)], recv_sem.at[3])
-    wait_bytes(recv_w.at[pl.ds(0, tm_size - 1)], recv_sem.at[5])
+    wait_bytes(recv_c.at[pl.ds(0, tm_size - 1)], recv_sem.at[3])
     wait_bytes(recv_g.at[pl.ds(0, tm_size - per)], recv_sem.at[4])
 
 
 def turn_back(
-    raw_layer, raw_gradw, raw_fgrad, layer_hbm, gradw_hbm, fgrad_hbm, raw, turned, load_sem, store_sem
+    coded_hbm, third_hbm, layer_hbm, gradw_hbm, fgrad_hbm, coded, third, turned, load_sem, store_sem
 ):
     channels, samples = turned.shape[2], turned.shape[1]
-    sources = [raw_layer, raw_gradw, raw_fgrad]
+    loads = [
+        pltpu.make_async_copy(coded_hbm, coded, load_sem.at[0]),
+        pltpu.make_async_copy(third_hbm, third, load_sem.at[1]),
+    ]
     targets = [layer_hbm, gradw_hbm, fgrad_hbm]
-    loads = [
-        pltpu.make_async_copy(sources[place], raw.at[place], load_sem.at[place])
-        for place in range(3)
-    ]
     stores = [
         pltpu.make_async_copy(turned.at[place], targets[place], store_sem.at[place])
         for place in range(3)
     ]
+
+    def turn(place, field):
+        turned[place] = field.reshape(channels, samples).T
+        stores[place].start()
+
     for load in loads:
         load.start()
-    for place in range(3):
-        loads[place].wait()
-        turned[place] = raw[place].reshape(channels, samples).T
-        stores[place].start()
+    loads[0].wait()
+    layer, gradw = decode_two(coded)
+    turn(0, layer)
+    turn(1, gradw)
+    loads[1].wait()
+    turn(2, third[...])
     for store in stores:
         store.wait()
 
@@ -385,12 +446,13 @@
     table = make_table(tm_size, samples)
     anywhere = pl.BlockSpec(memory_space=pl.ANY)
     block = jax.ShapeDtypeStruct((samples, channels), F32)
+    coded = jax.ShapeDtypeStruct((tm_size, PACK + 1, samples), jnp.int32)
     pieces = jax.ShapeDtypeStruct((tm_size, PACK, samples), F32)
     received = pl.pallas_call(
         functools.partial(kernel, tm_size, dp_size),
-        out_shape=[pieces] * 3,
+        out_shape=[coded, pieces],
         in_specs=[anywhere] * 8,
-        out_specs=[anywhere] * 3,
+        out_specs=[anywhere] * 2,
         scratch_shapes=[
             pltpu.SMEM((1,), jnp.int32),
             pltpu.VMEM((samples, channels), BF16),
@@ -400,18 +462,16 @@
             pltpu.VMEM((1, channels), F32),
             pltpu.VMEM((speaker_table.shape[0] // ROWS16, ROWS16, channels), BF16),
             pltpu.VMEM(table.shape, F32),
-            pltpu.VMEM((2 * rows, rows), BF16),
-            pltpu.VMEM((2 * rows, rows), BF16),
+            *[pltpu.VMEM((rows, rows), BF16)] * 4,
             pltpu.VMEM((2 * samples, 2 * samples), BF16),
             pltpu.VMEM((2 * samples, 2 * samples), BF16),
             pltpu.VMEM((tm_size, 2 * PACK, samples), BF16),
             pltpu.VMEM((tm_size, 2 * PACK, samples), BF16),
-            pltpu.VMEM((tm_size, PACK, samples), F32),
-            pltpu.VMEM((tm_size, PACK, samples), F32),
-            pltpu.VMEM((tm_size, PACK, samples), F32),
-            pltpu.VMEM((tm_size, PACK, samples), F32),
-            pltpu.VMEM((tm_size, PACK, samples), F32),
-            pltpu.VMEM((tm_size, PACK, samples), F32),
+            pltpu.VMEM((tm_size, PACK // 2 + 1, samples), jnp.int32),
+            pltpu.VMEM((tm_size, PACK // 2 + 1, samples), jnp.int32),
+            pltpu.VMEM((tm_size, PACK + 1, samples), jnp.int32),
+            pltpu.VMEM((tm_size, PACK // 2 + 1, samples), jnp.int32),
+            pltpu.VMEM((tm_size, PACK // 2 + 1, samples), jnp.int32),
             pltpu.VMEM((per, PACK, samples), F32),
             pltpu.SemaphoreType.DMA((11,)),
             pltpu.SemaphoreType.DMA((6,)),
@@ -434,12 +494,13 @@
     layer_out, grad_waveform, filter_grad = pl.pallas_call(
         turn_back,
         out_shape=[block, block, block],
-        in_specs=[anywhere] * 3,
+        in_specs=[anywhere] * 2,
         out_specs=[anywhere] * 3,
         scratch_shapes=[
-            pltpu.VMEM((3, tm_size, PACK, samples), F32),
+            pltpu.VMEM(coded.shape, jnp.int32),
+            pltpu.VMEM(pieces.shape, F32),
             pltpu.VMEM((3, samples, channels), F32),
-            pltpu.SemaphoreType.DMA((3,)),
+            pltpu.SemaphoreType.DMA((2,)),
             pltpu.SemaphoreType.DMA((3,)),
         ],
         compiler_params=pltpu.CompilerParams(vmem_limit_bytes=62 * 1024 * 1024),

time: 35.5 us -> 33.9 us (0.955)
  Pallas kernels: 34.1 us -> 32.4 us
    pallas_call x1, Pallas kernels: 32.2 us -> 30.5 us  [local(): pl.pallas_call(functools.partial(kernel, tm_size, dp_size), out_shape=[co...]
where the time goes in v4:
time: 33.9 us; the launch traced here: 33.7 us
  Pallas kernels  32.4 us (96%)
  between operations  1.29 us (4%)
    pallas_call x1, Pallas kernels, local(): pl.pallas_call(functools.partial(kernel, tm_size, dp_size), out_shape=[co...  30.5 us
    pallas_call x1, Pallas kernels, local(): pl.pallas_call(turn_back, out_shape=[block, block, block], in_specs=[anyw...  1.96 us

profile of v4, /device:TPU:1, one launch (start us, length us, event | category | flops | bytes accessed | tf_op | source)
XLA Modules:
  0.0 33.7 jit_solution(10386705535411178148)
XLA Ops:
  1.3 30.5 %shard_map.103 = (s32[32,9,128]{2,1,0:T(8,128)}, f32[32,8,128]{2,1,0:T(8,128)}) custom-call(s32[1]{0:T(128)S(6)} %copy.11.ids_hbm, bf16[128,256]{1,0:T(8,128)(2,1)} %bitcast.7, bf16[128,256]{1,0:T(8,128)(2,1)} %bitcast.8, f32[128,256]{1,0:T(8,128)} %filt_hbm.1, f32[3,256]{1,0:T(4,128)} %taps_hbm.1, f32[1,256]{1,0:T(1,128)} %bitcast.9, ...), custom_call_target="tpu_custom_call" | custom-call | tf_op jit(solution)/shard_map/pallas_call | solution.py:451
  31.8 2.0 %shard_map.104 = (f32[128,256]{1,0:T(8,128)}, f32[128,256]{1,0:T(8,128)}, f32[128,256]{1,0:T(8,128)}) custom-call(s32[32,9,128]{2,1,0:T(8,128)} %get-tuple-element.8.coded_hbm, f32[32,8,128]{2,1,0:T(8,128)} %get-tuple-element.9.third_hbm), custom_call_target="tpu_custom_call" | custom-call | tf_op jit(solution)/shard_map/pallas_call | solution.py:494

commit v5 on v4

--- a/solution.py
+++ b/solution.py
@@ -138,7 +138,8 @@
     gain_hbm,
     speakers_hbm,
     table_hbm,
-    recv_c,
+    layer_hbm,
+    gradw_hbm,
     recv_g,
     ids,
     wave_ref,
@@ -159,6 +160,8 @@
     send_f,
     recv_f,
     send_c,
+    recv_c,
+    turned,
     send_r,
     recv_r,
     send_g,
@@ -318,7 +321,7 @@
     mixed_value = mixed[:, :samples] + dot(lh[...], value_low)
     mixed = jnp.concatenate([mixed_value, mixed[:, samples:]], axis=1)
     (vr, vi), (gr, gi) = forward(mixed)
-    encode_one(to_blocks(backward([(vr * gr + vi * gi, vr * gi - vi * gr)])), send_r)
+    send_r[...] = to_blocks(backward([(vr * gr + vi * gi, vr * gi - vi * gr)]))
 
     @pl.when(adder != dp)
     def _():
@@ -336,13 +339,13 @@
             device_id_type=MESH,
         ).start()
 
-    @pl.loop(0, tm_size - 1)
+    @pl.loop(0, tm_size)
     def _(step):
-        send_partial(tm_peer(step))
-
-    @pl.when(adder != dp)
-    def _():
-        send_partial(tm)
+        block = lax.rem(place + far_first(lax.rem(step, per), per), per) * dp_size + lax.div(step, per)
+
+        @pl.when(jnp.logical_not((block == tm) & (adder == dp)))
+        def _():
+            send_partial(block)
 
     @pl.when(adder == dp)
     def _():
@@ -361,9 +364,22 @@
     layer = to_blocks(convolved) + gain * value
     middle = (to_blocks(correlated) + gain * grad) * scale
     encode_two(layer, stencil(middle, taps[::-1]), send_c)
-    exchange(send_c, recv_c, 3)
-    own_c = pltpu.make_async_copy(send_c.at[tm], recv_c.at[tm], local_sem.at[8])
-    own_c.start()
+    @pl.loop(0, tm_size)
+    def _(step):
+        peer = lax.rem(place + far_first(lax.rem(step, per), per), per) * dp_size + lax.div(step, per)
+
+        @pl.when(peer != tm)
+        def _():
+            pltpu.make_async_remote_copy(
+                src_ref=send_c.at[peer],
+                dst_ref=recv_c.at[tm],
+                send_sem=send_sem.at[3],
+                recv_sem=recv_sem.at[3],
+                device_id=(dp, peer),
+                device_id_type=MESH,
+            ).start()
+
+    recv_c[tm] = send_c[tm]
 
     @pl.when(adder == dp)
     def _():
@@ -373,7 +389,7 @@
     def _():
         wait_bytes(recv_r, recv_sem.at[2])
 
-    send_g[...] = jnp.sum(decode_one(recv_r).reshape(dp_size, per, PACK, samples), axis=0)
+    send_g[...] = jnp.sum(recv_r[...].reshape(dp_size, per, PACK, samples), axis=0)
     summed = recv_g.at[pl.ds(dp * per, per)]
 
     @pl.loop(0, dp_size - 1)
@@ -389,6 +405,14 @@
 
     own_g = pltpu.make_async_copy(send_g, summed, local_sem.at[9])
     own_g.start()
+    wait_bytes(recv_c.at[pl.ds(0, tm_size - 1)], recv_sem.at[3])
+    stores = []
+    for place_out, (field, target) in enumerate(zip(decode_two(recv_c), (layer_hbm, gradw_hbm))):
+        turned[place_out] = field.reshape(channels, samples).T
+        stores.append(
+            pltpu.make_async_copy(turned.at[place_out], target, local_sem.at[8 + 2 * place_out])
+        )
+        stores[-1].start()
     wait_bytes(send_a.at[pl.ds(0, tm_size - 1)], send_sem.at[0])
     wait_bytes(send_f.at[pl.ds(0, tm_size - 1)], send_sem.at[1])
     wait_bytes(send_c.at[pl.ds(0, tm_size - 1)], send_sem.at[3])
@@ -402,38 +426,34 @@
         wait_bytes(send_r, send_sem.at[2])
 
     wait_bytes(recv_g.at[pl.ds(0, tm_size - per)], send_sem.at[4])
-    own_c.wait()
+    for store in stores:
+        store.wait()
     own_g.wait()
-    wait_bytes(recv_c.at[pl.ds(0, tm_size - 1)], recv_sem.at[3])
     wait_bytes(recv_g.at[pl.ds(0, tm_size - per)], recv_sem.at[4])
 
 
-def turn_back(
-    coded_hbm, third_hbm, layer_hbm, gradw_hbm, fgrad_hbm, coded, third, turned, load_sem, store_sem
+def finish(
+    layer_in, gradw_in, third_hbm, layer_hbm, gradw_hbm, fgrad_hbm, clips, third, turned, load_sem, store_sem
 ):
-    channels, samples = turned.shape[2], turned.shape[1]
+    channels, samples = turned.shape[1], turned.shape[0]
     loads = [
-        pltpu.make_async_copy(coded_hbm, coded, load_sem.at[0]),
-        pltpu.make_async_copy(third_hbm, third, load_sem.at[1]),
+        pltpu.make_async_copy(third_hbm, third, load_sem.at[2]),
+        pltpu.make_async_copy(layer_in, clips.at[0], load_sem.at[0]),
+        pltpu.make_async_copy(gradw_in, clips.at[1], load_sem.at[1]),
     ]
-    targets = [layer_hbm, gradw_hbm, fgrad_hbm]
     stores = [
-        pltpu.make_async_copy(turned.at[place], targets[place], store_sem.at[place])
-        for place in range(3)
+        pltpu.make_async_copy(turned, fgrad_hbm, store_sem.at[2]),
+        pltpu.make_async_copy(clips.at[0], layer_hbm, store_sem.at[0]),
+        pltpu.make_async_copy(clips.at[1], gradw_hbm, store_sem.at[1]),
     ]
-
-    def turn(place, field):
-        turned[place] = field.reshape(channels, samples).T
-        stores[place].start()
-
     for load in loads:
         load.start()
     loads[0].wait()
-    layer, gradw = decode_two(coded)
-    turn(0, layer)
-    turn(1, gradw)
-    loads[1].wait()
-    turn(2, third[...])
+    turned[...] = third[...].reshape(channels, samples).T
+    stores[0].start()
+    for place in (1, 2):
+        loads[place].wait()
+        stores[place].start()
     for store in stores:
         store.wait()
 
@@ -446,13 +466,12 @@
     table = make_table(tm_size, samples)
     anywhere = pl.BlockSpec(memory_space=pl.ANY)
     block = jax.ShapeDtypeStruct((samples, channels), F32)
-    coded = jax.ShapeDtypeStruct((tm_size, PACK + 1, samples), jnp.int32)
     pieces = jax.ShapeDtypeStruct((tm_size, PACK, samples), F32)
     received = pl.pallas_call(
         functools.partial(kernel, tm_size, dp_size),
-        out_shape=[coded, pieces],
+        out_shape=[block, block, pieces],
         in_specs=[anywhere] * 8,
-        out_specs=[anywhere] * 2,
+        out_specs=[anywhere] * 3,
         scratch_shapes=[
             pltpu.SMEM((1,), jnp.int32),
             pltpu.VMEM((samples, channels), BF16),
@@ -470,8 +489,10 @@
             pltpu.VMEM((tm_size, PACK // 2 + 1, samples), jnp.int32),
             pltpu.VMEM((tm_size, PACK // 2 + 1, samples), jnp.int32),
             pltpu.VMEM((tm_size, PACK + 1, samples), jnp.int32),
-            pltpu.VMEM((tm_size, PACK // 2 + 1, samples), jnp.int32),
-            pltpu.VMEM((tm_size, PACK // 2 + 1, samples), jnp.int32),
+            pltpu.VMEM((tm_size, PACK + 1, samples), jnp.int32),
+            pltpu.VMEM((2, samples, channels), F32),
+            pltpu.VMEM((tm_size, PACK, samples), F32),
+            pltpu.VMEM((tm_size, PACK, samples), F32),
             pltpu.VMEM((per, PACK, samples), F32),
             pltpu.SemaphoreType.DMA((11,)),
             pltpu.SemaphoreType.DMA((6,)),
@@ -492,15 +513,15 @@
         jnp.asarray(table),
     )
     layer_out, grad_waveform, filter_grad = pl.pallas_call(
-        turn_back,
+        finish,
         out_shape=[block, block, block],
-        in_specs=[anywhere] * 2,
+        in_specs=[anywhere] * 3,
         out_specs=[anywhere] * 3,
         scratch_shapes=[
-            pltpu.VMEM(coded.shape, jnp.int32),
+            pltpu.VMEM((2, samples, channels), F32),
             pltpu.VMEM(pieces.shape, F32),
-            pltpu.VMEM((3, samples, channels), F32),
-            pltpu.SemaphoreType.DMA((2,)),
+            pltpu.VMEM((samples, channels), F32),
+            pltpu.SemaphoreType.DMA((3,)),
             pltpu.SemaphoreType.DMA((3,)),
         ],
         compiler_params=pltpu.CompilerParams(vmem_limit_bytes=62 * 1024 * 1024),

time: 33.9 us -> 32.8 us (0.968)
  Pallas kernels: 32.4 us -> 31.4 us
    pallas_call x2, Pallas kernels: 32.4 us -> 31.4 us  [the longest x1 29.6 us: local(): pl.pallas_call(functools.partial(kernel, tm_size, dp_size), out_shape=[bl...]
where the time goes in v5:
time: 32.8 us; the launch traced here: 32.7 us
  Pallas kernels  31.4 us (96%)
  between operations  1.29 us (4%)
    pallas_call x1, Pallas kernels, local(): pl.pallas_call(functools.partial(kernel, tm_size, dp_size), out_shape=[bl...  29.6 us
    pallas_call x1, Pallas kernels, local(): pl.pallas_call(finish, out_shape=[block, block, block], in_specs=[anywher...  1.8 us

profile of v5, /device:TPU:1, one launch (start us, length us, event | category | flops | bytes accessed | tf_op | source)
XLA Modules:
  0.0 32.7 jit_solution(5657731255304753509)
XLA Ops:
  1.3 29.6 %shard_map.103 = (f32[128,256]{1,0:T(8,128)}, f32[128,256]{1,0:T(8,128)}, f32[32,8,128]{2,1,0:T(8,128)}) custom-call(s32[1]{0:T(128)S(6)} %copy.11.ids_hbm, bf16[128,256]{1,0:T(8,128)(2,1)} %bitcast.7, bf16[128,256]{1,0:T(8,128)(2,1)} %bitcast.8, f32[128,256]{1,0:T(8,128)} %filt_hbm.1, f32[3,256]{1,0:T(4,128)} %taps_hbm.1, f32[1,256]{1,0:T(1,128)} %bitcast.9, ...), custom_call_target="tpu_custom_call" | custom-call | tf_op jit(solution)/shard_map/pallas_call | solution.py:470
  30.9 1.8 %shard_map.104 = (f32[128,256]{1,0:T(8,128)}, f32[128,256]{1,0:T(8,128)}, f32[128,256]{1,0:T(8,128)}) custom-call(f32[128,256]{1,0:T(8,128)} %get-tuple-element.9.layer_in, f32[128,256]{1,0:T(8,128)} %get-tuple-element.10.gradw_in, f32[32,8,128]{2,1,0:T(8,128)} %get-tuple-element.11.third_hbm), custom_call_target="tpu_custom_call" | custom-call | tf_op jit(solution)/shard_map/pallas_call | solution.py:515

commit v6 on v5

--- a/solution.py
+++ b/solution.py
@@ -109,6 +109,14 @@
     first_power = (powers & 1023).astype(F32)
     second_power = (powers >> 10).astype(F32)
     return first_of(words) * step_size(first_power), second_of(words) * step_size(second_power)
+
+
+def adders(size):
+    return [4, 2, 5, 3, 6, 0, 7, 1] if size == 8 else list(range(size))
+
+
+def pick(values, index):
+    return sum(jnp.where(index == place, int(value), 0) for place, value in enumerate(values))
 
 
 def far_first(step, size):
@@ -179,24 +187,6 @@
     channels = wave_ref.shape[1]
     rows = tm_size * PACK
 
-    barrier = pltpu.get_barrier_semaphore()
-
-    def tm_peer(step):
-        far = far_first(lax.div(step, per), dp_size)
-        across = far_first(lax.rem(step, per), per)
-        return lax.rem(place + across, per) * dp_size + lax.rem(column_at + far, dp_size)
-
-    def dp_peer(step):
-        return lax.rem(dp + far_first(step, dp_size), dp_size)
-
-    @pl.loop(0, tm_size - 1)
-    def _(step):
-        pl.semaphore_signal(barrier, inc=1, device_id=(dp, tm_peer(step)), device_id_type=MESH)
-
-    @pl.loop(0, dp_size - 1)
-    def _(step):
-        pl.semaphore_signal(barrier, inc=1, device_id=(dp_peer(step), tm), device_id_type=MESH)
-
     pairs = [
         (wave_hbm, wave_ref),
         (cot_hbm, cot_ref),
@@ -212,6 +202,27 @@
         for slot, (source, target) in enumerate(pairs)
     ]
 
+    for load in loads[:3]:
+        load.start()
+
+    barrier = pltpu.get_barrier_semaphore()
+
+    def tm_peer(step):
+        far = far_first(lax.div(step, per), dp_size)
+        across = far_first(lax.rem(step, per), per)
+        return lax.rem(place + across, per) * dp_size + lax.rem(column_at + far, dp_size)
+
+    def dp_peer(step):
+        return lax.rem(dp + far_first(step, dp_size), dp_size)
+
+    @pl.loop(0, tm_size - 1)
+    def _(step):
+        pl.semaphore_signal(barrier, inc=1, device_id=(dp, tm_peer(step)), device_id_type=MESH)
+
+    @pl.loop(0, dp_size - 1)
+    def _(step):
+        pl.semaphore_signal(barrier, inc=1, device_id=(dp_peer(step), tm), device_id_type=MESH)
+
     def wait_bytes(like, sem):
         pltpu.make_async_copy(like, like, sem).wait()
 
@@ -231,8 +242,6 @@
     def to_blocks(field):
         return field.reshape(tm_size, PACK, samples)
 
-    for load in loads[:3]:
-        load.start()
     loads[0].wait()
     wave_t = to_blocks(wave_ref[...].astype(F32).T)
     loads[1].wait()
@@ -242,18 +251,14 @@
     exchange(send_a, recv_a, 0)
     recv_a[tm] = send_a[tm]
 
-    adder = lax.div(tm, per)
+    adder = pick(adders(dp_size), lax.div(tm, per))
+    share = pick(np.argsort(adders(dp_size)), dp)
 
     @pl.when(adder == dp)
     def _():
         @pl.loop(0, dp_size - 1)
         def _(step):
             pl.semaphore_signal(plane_sem, inc=1, device_id=(dp_peer(step), tm), device_id_type=MESH)
-
-    loads[2].wait()
-    encode_one(to_blocks(filt_ref[...].T), send_f)
-    exchange(send_f, recv_f, 1)
-    recv_f[tm] = send_f[tm]
 
     for load in loads[3:]:
         load.start()
@@ -264,6 +269,11 @@
     rh[...], rl[...] = split(table[2 * rows : 2 * rows + 2 * samples, : 2 * samples])
     tc = table[2 * rows + 2 * samples :, :samples]
     ts = table[2 * rows + 2 * samples :, samples : 2 * samples]
+    loads[2].wait()
+    encode_one(to_blocks(filt_ref[...].T), send_f)
+    exchange(send_f, recv_f, 1)
+    recv_f[tm] = send_f[tm]
+
     lane = lax.broadcasted_iota(jnp.int32, (PACK, channels), 1)
     row = lax.broadcasted_iota(jnp.int32, (PACK, channels), 0)
     mine = lane == tm * PACK + row
@@ -339,11 +349,15 @@
             device_id_type=MESH,
         ).start()
 
+    @pl.when(jnp.logical_not((tm == 0) & (adder == dp)))
+    def _():
+        send_partial(0)
+
     @pl.loop(0, tm_size)
     def _(step):
         block = lax.rem(place + far_first(lax.rem(step, per), per), per) * dp_size + lax.div(step, per)
 
-        @pl.when(jnp.logical_not((block == tm) & (adder == dp)))
+        @pl.when((block != 0) & jnp.logical_not((block == tm) & (adder == dp)))
         def _():
             send_partial(block)
 
@@ -390,7 +404,7 @@
         wait_bytes(recv_r, recv_sem.at[2])
 
     send_g[...] = jnp.sum(recv_r[...].reshape(dp_size, per, PACK, samples), axis=0)
-    summed = recv_g.at[pl.ds(dp * per, per)]
+    summed = recv_g.at[pl.ds(share * per, per)]
 
     @pl.loop(0, dp_size - 1)
     def _(step):

time: 32.8 us -> 31.7 us (0.966)
  Pallas kernels: 31.4 us -> 30.2 us
    pallas_call x1, Pallas kernels: 29.6 us -> 28.4 us  [local(): pl.pallas_call(functools.partial(kernel, tm_size, dp_size), out_shape=[bl...]
where the time goes in v6:
time: 31.7 us; the launch traced here: 31.5 us
  Pallas kernels  30.2 us (95%)
  between operations  1.29 us (4%)
    pallas_call x1, Pallas kernels, local(): pl.pallas_call(functools.partial(kernel, tm_size, dp_size), out_shape=[bl...  28.4 us
    pallas_call x1, Pallas kernels, local(): pl.pallas_call(finish, out_shape=[block, block, block], in_specs=[anywher...  1.8 us

profile of v6, /device:TPU:1, one launch (start us, length us, event | category | flops | bytes accessed | tf_op | source)
XLA Modules:
  0.0 31.5 jit_solution(17576116572540634088)
XLA Ops:
  1.3 28.4 %shard_map.103 = (f32[128,256]{1,0:T(8,128)}, f32[128,256]{1,0:T(8,128)}, f32[32,8,128]{2,1,0:T(8,128)}) custom-call(s32[1]{0:T(128)S(6)} %copy.11.ids_hbm, bf16[128,256]{1,0:T(8,128)(2,1)} %bitcast.7, bf16[128,256]{1,0:T(8,128)(2,1)} %bitcast.8, f32[128,256]{1,0:T(8,128)} %filt_hbm.1, f32[3,256]{1,0:T(4,128)} %taps_hbm.1, f32[1,256]{1,0:T(1,128)} %bitcast.9, ...), custom_call_target="tpu_custom_call" | custom-call | tf_op jit(solution)/shard_map/pallas_call | solution.py:484
  29.7 1.8 %shard_map.104 = (f32[128,256]{1,0:T(8,128)}, f32[128,256]{1,0:T(8,128)}, f32[128,256]{1,0:T(8,128)}) custom-call(f32[128,256]{1,0:T(8,128)} %get-tuple-element.9.layer_in, f32[128,256]{1,0:T(8,128)} %get-tuple-element.10.gradw_in, f32[32,8,128]{2,1,0:T(8,128)} %get-tuple-element.11.third_hbm), custom_call_target="tpu_custom_call" | custom-call | tf_op jit(solution)/shard_map/pallas_call | solution.py:529

commit v7 on v6

--- a/solution.py
+++ b/solution.py
@@ -146,8 +146,8 @@
     gain_hbm,
     speakers_hbm,
     table_hbm,
-    layer_hbm,
-    gradw_hbm,
+    layer_ref,
+    gradw_ref,
     recv_g,
     ids,
     wave_ref,
@@ -169,7 +169,6 @@
     recv_f,
     send_c,
     recv_c,
-    turned,
     send_r,
     recv_r,
     send_g,
@@ -420,13 +419,9 @@
     own_g = pltpu.make_async_copy(send_g, summed, local_sem.at[9])
     own_g.start()
     wait_bytes(recv_c.at[pl.ds(0, tm_size - 1)], recv_sem.at[3])
-    stores = []
-    for place_out, (field, target) in enumerate(zip(decode_two(recv_c), (layer_hbm, gradw_hbm))):
-        turned[place_out] = field.reshape(channels, samples).T
-        stores.append(
-            pltpu.make_async_copy(turned.at[place_out], target, local_sem.at[8 + 2 * place_out])
-        )
-        stores[-1].start()
+    layer, gradw = decode_two(recv_c)
+    layer_ref[...] = layer.reshape(channels, samples).T
+    gradw_ref[...] = gradw.reshape(channels, samples).T
     wait_bytes(send_a.at[pl.ds(0, tm_size - 1)], send_sem.at[0])
     wait_bytes(send_f.at[pl.ds(0, tm_size - 1)], send_sem.at[1])
     wait_bytes(send_c.at[pl.ds(0, tm_size - 1)], send_sem.at[3])
@@ -440,34 +435,21 @@
         wait_bytes(send_r, send_sem.at[2])
 
     wait_bytes(recv_g.at[pl.ds(0, tm_size - per)], send_sem.at[4])
-    for store in stores:
-        store.wait()
     own_g.wait()
     wait_bytes(recv_g.at[pl.ds(0, tm_size - per)], recv_sem.at[4])
 
 
-def finish(
-    layer_in, gradw_in, third_hbm, layer_hbm, gradw_hbm, fgrad_hbm, clips, third, turned, load_sem, store_sem
-):
+def finish(layer_in, gradw_in, third, layer_hbm, gradw_hbm, fgrad_hbm, turned, store_sem):
     channels, samples = turned.shape[1], turned.shape[0]
-    loads = [
-        pltpu.make_async_copy(third_hbm, third, load_sem.at[2]),
-        pltpu.make_async_copy(layer_in, clips.at[0], load_sem.at[0]),
-        pltpu.make_async_copy(gradw_in, clips.at[1], load_sem.at[1]),
+    stores = [
+        pltpu.make_async_copy(layer_in, layer_hbm, store_sem.at[0]),
+        pltpu.make_async_copy(gradw_in, gradw_hbm, store_sem.at[1]),
+        pltpu.make_async_copy(turned, fgrad_hbm, store_sem.at[2]),
     ]
-    stores = [
-        pltpu.make_async_copy(turned, fgrad_hbm, store_sem.at[2]),
-        pltpu.make_async_copy(clips.at[0], layer_hbm, store_sem.at[0]),
-        pltpu.make_async_copy(clips.at[1], gradw_hbm, store_sem.at[1]),
-    ]
-    for load in loads:
-        load.start()
-    loads[0].wait()
+    stores[0].start()
+    stores[1].start()
     turned[...] = third[...].reshape(channels, samples).T
-    stores[0].start()
-    for place in (1, 2):
-        loads[place].wait()
-        stores[place].start()
+    stores[2].start()
     for store in stores:
         store.wait()
 
@@ -479,13 +461,14 @@
     rows = tm_size * PACK
     table = make_table(tm_size, samples)
     anywhere = pl.BlockSpec(memory_space=pl.ANY)
+    vmem = pl.BlockSpec(memory_space=pltpu.VMEM)
     block = jax.ShapeDtypeStruct((samples, channels), F32)
     pieces = jax.ShapeDtypeStruct((tm_size, PACK, samples), F32)
     received = pl.pallas_call(
         functools.partial(kernel, tm_size, dp_size),
-        out_shape=[block, block, pieces],
+        out_shape=[pltpu.VMEM(block.shape, F32)] * 2 + [pltpu.VMEM(pieces.shape, F32)],
         in_specs=[anywhere] * 8,
-        out_specs=[anywhere] * 3,
+        out_specs=[vmem] * 3,
         scratch_shapes=[
             pltpu.SMEM((1,), jnp.int32),
             pltpu.VMEM((samples, channels), BF16),
@@ -504,7 +487,6 @@
             pltpu.VMEM((tm_size, PACK // 2 + 1, samples), jnp.int32),
             pltpu.VMEM((tm_size, PACK + 1, samples), jnp.int32),
             pltpu.VMEM((tm_size, PACK + 1, samples), jnp.int32),
-            pltpu.VMEM((2, samples, channels), F32),
             pltpu.VMEM((tm_size, PACK, samples), F32),
             pltpu.VMEM((tm_size, PACK, samples), F32),
             pltpu.VMEM((per, PACK, samples), F32),
@@ -514,31 +496,33 @@
             pltpu.SemaphoreType.REGULAR,
         ],
         compiler_params=pltpu.CompilerParams(
-            collective_id=0, has_side_effects=True, vmem_limit_bytes=62 * 1024 * 1024
+            collective_id=0, has_side_effects=True, vmem_limit_bytes=32 * 1024 * 1024
         ),
     )(
         speaker_ids,
-        waveform[0],
-        cotangent[0],
-        filters,
-        stencil_taps,
-        skip_gain[None],
-        speaker_table.reshape(-1, ROWS16, channels),
-        jnp.asarray(table),
+        *[
+            pltpu.with_memory_space_constraint(operand, pltpu.HBM)
+            for operand in (
+                waveform[0],
+                cotangent[0],
+                filters,
+                stencil_taps,
+                skip_gain[None],
+                speaker_table.reshape(-1, ROWS16, channels),
+                jnp.asarray(table),
+            )
+        ]
     )
     layer_out, grad_waveform, filter_grad = pl.pallas_call(
         finish,
         out_shape=[block, block, block],
-        in_specs=[anywhere] * 3,
+        in_specs=[vmem] * 3,
         out_specs=[anywhere] * 3,
         scratch_shapes=[
-            pltpu.VMEM((2, samples, channels), F32),
-            pltpu.VMEM(pieces.shape, F32),
             pltpu.VMEM((samples, channels), F32),
             pltpu.SemaphoreType.DMA((3,)),
-            pltpu.SemaphoreType.DMA((3,)),
         ],
-        compiler_params=pltpu.CompilerParams(vmem_limit_bytes=62 * 1024 * 1024),
+        compiler_params=pltpu.CompilerParams(vmem_limit_bytes=16 * 1024 * 1024),
     )(*received)
     return layer_out[None], grad_waveform[None], filter_grad
 

time: 31.7 us -> 30.5 us (0.962)
  Pallas kernels: 30.2 us -> 29.1 us
    pallas_call x2, Pallas kernels: 30.2 us -> 29.1 us  [the longest x1 28.3 us: local(): pl.pallas_call(functools.partial(kernel, tm_size, dp_size), out_shape=[pl...]
where the time goes in v7:
time: 30.5 us; the launch traced here: 30.4 us
  Pallas kernels  29.1 us (95%)
  between operations  1.29 us (4%)
    pallas_call x1, Pallas kernels, local(): pl.pallas_call(functools.partial(kernel, tm_size, dp_size), out_shape=[pl...  28.3 us
    pallas_call x1, Pallas kernels, local(): pl.pallas_call(finish, out_shape=[block, block, block], in_specs=[vmem] *...  0.78 us

profile of v7, /device:TPU:1, one launch (start us, length us, event | category | flops | bytes accessed | tf_op | source)
XLA Modules:
  0.0 30.4 jit_solution(4910718946558552666)
XLA Ops:
  1.3 28.3 %shard_map.103 = (f32[128,256]{1,0:T(8,128)S(1)}, f32[128,256]{1,0:T(8,128)S(1)}, f32[32,8,128]{2,1,0:T(8,128)S(1)}) custom-call(s32[1]{0:T(128)S(6)} %copy.11.ids_hbm, bf16[128,256]{1,0:T(8,128)(2,1)} %bitcast.7, bf16[128,256]{1,0:T(8,128)(2,1)} %bitcast.8, f32[128,256]{1,0:T(8,128)} %filt_hbm.1, f32[3,256]{1,0:T(4,128)} %taps_hbm.1, f32[1,256]{1,0:T(1,128)} %bitcast.9, ...), custom_call_target="tpu_custom_call" | custom-call | tf_op jit(solution)/shard_map/pallas_call | solution.py:467
  29.6 0.8 %shard_map.104 = (f32[128,256]{1,0:T(8,128)}, f32[128,256]{1,0:T(8,128)}, f32[128,256]{1,0:T(8,128)}) custom-call(f32[128,256]{1,0:T(8,128)S(1)} %get-tuple-element.9.layer_in, f32[128,256]{1,0:T(8,128)S(1)} %get-tuple-element.10.gradw_in, f32[32,8,128]{2,1,0:T(8,128)S(1)} %get-tuple-element.11.third), custom_call_target="tpu_custom_call" | custom-call | tf_op jit(solution)/shard_map/pallas_call | solution.py:516

commit v8 on v7

--- a/solution.py
+++ b/solution.py
@@ -228,7 +228,7 @@
     def exchange(source, target, which):
         @pl.loop(0, tm_size - 1)
         def _(step):
-            peer = tm_peer(step)
+            peer = tm_peer(lax.rem(step + 15 * lax.rem(dp, 2), tm_size - 1))
             pltpu.make_async_remote_copy(
                 src_ref=source.at[peer],
                 dst_ref=target.at[tm],
@@ -288,6 +288,12 @@
     taps = [column(taps_ref[place : place + 1, :]) for place in range(3)]
     gain = column(gain_ref[...])
 
+    def left_mix(table_high, table_low, field):
+        high, low = split(field)
+        columns = field.shape[1]
+        both = dot(table_high[...], jnp.concatenate([high, low], axis=1))
+        return both[:, :columns] + (both[:, columns:] + dot(table_low[...], high))
+
     def right_mix(field):
         high, low = split(field)
         return dot(high, rh[...]) + (dot(high, rl[...]) + dot(low, rh[...]))
@@ -317,8 +323,7 @@
             part = inner[field * half_rows : (field + 1) * half_rows]
             real, imag = twiddle(part[:, :samples], part[:, samples:])
             turned.append(jnp.concatenate([real, imag[PACK:-PACK]], axis=0))
-        high, low = split(jnp.concatenate(turned, axis=1))
-        return dot(bh[...], high) + (dot(bl[...], high) + dot(bh[...], low))
+        return left_mix(bh, bl, jnp.concatenate(turned, axis=1))
 
     wait_bytes(recv_a.at[pl.ds(0, tm_size - 1)], recv_sem.at[0])
     both = recv_a[...].astype(F32)
@@ -354,7 +359,7 @@
 
     @pl.loop(0, tm_size)
     def _(step):
-        block = lax.rem(place + far_first(lax.rem(step, per), per), per) * dp_size + lax.div(step, per)
+        block = lax.rem(step, per) * dp_size + lax.div(step, per)
 
         @pl.when((block != 0) & jnp.logical_not((block == tm) & (adder == dp)))
         def _():
@@ -365,8 +370,7 @@
         recv_r[slot] = send_r[tm]
 
     wait_bytes(recv_f.at[pl.ds(0, tm_size - 1)], recv_sem.at[1])
-    high, low = split(decode_one(recv_f).reshape(rows, samples))
-    ((fr, fi),) = forward(dot(lh[...], high) + (dot(ll[...], high) + dot(lh[...], low)))
+    ((fr, fi),) = forward(left_mix(lh, ll, decode_one(recv_f).reshape(rows, samples)))
     results = backward(
         [
             (vr * fr - vi * fi, vr * fi + vi * fr),

time: 30.5 us -> 30.5 us (level)
  no operation moved by 1% of the time
where the time goes in v8:
time: 30.5 us; the launch traced here: 30.3 us
  Pallas kernels  29 us (95%)
  between operations  1.29 us (4%)
    pallas_call x1, Pallas kernels, local(): pl.pallas_call(functools.partial(kernel, tm_size, dp_size), out_shape=[pl...  28.2 us
    pallas_call x1, Pallas kernels, local(): pl.pallas_call(finish, out_shape=[block, block, block], in_specs=[vmem] *...  0.78 us

profile of v8, /device:TPU:1, one launch (start us, length us, event | category | flops | bytes accessed | tf_op | source)
XLA Modules:
  0.0 30.3 jit_solution(11944769183403085977)
XLA Ops:
  1.3 28.2 %shard_map.103 = (f32[128,256]{1,0:T(8,128)S(1)}, f32[128,256]{1,0:T(8,128)S(1)}, f32[32,8,128]{2,1,0:T(8,128)S(1)}) custom-call(s32[1]{0:T(128)S(6)} %copy.11.ids_hbm, bf16[128,256]{1,0:T(8,128)(2,1)} %bitcast.7, bf16[128,256]{1,0:T(8,128)(2,1)} %bitcast.8, f32[128,256]{1,0:T(8,128)} %filt_hbm.1, f32[3,256]{1,0:T(4,128)} %taps_hbm.1, f32[1,256]{1,0:T(1,128)} %bitcast.9, ...), custom_call_target="tpu_custom_call" | custom-call | tf_op jit(solution)/shard_map/pallas_call | solution.py:471
  29.5 0.8 %shard_map.104 = (f32[128,256]{1,0:T(8,128)}, f32[128,256]{1,0:T(8,128)}, f32[128,256]{1,0:T(8,128)}) custom-call(f32[128,256]{1,0:T(8,128)S(1)} %get-tuple-element.9.layer_in, f32[128,256]{1,0:T(8,128)S(1)} %get-tuple-element.10.gradw_in, f32[32,8,128]{2,1,0:T(8,128)S(1)} %get-tuple-element.11.third), custom_call_target="tpu_custom_call" | custom-call | tf_op jit(solution)/shard_map/pallas_call | solution.py:520

commit v9 on v8

--- a/solution.py
+++ b/solution.py
@@ -201,8 +201,6 @@
         for slot, (source, target) in enumerate(pairs)
     ]
 
-    for load in loads[:3]:
-        load.start()
 
     barrier = pltpu.get_barrier_semaphore()
 
@@ -221,6 +219,9 @@
     @pl.loop(0, dp_size - 1)
     def _(step):
         pl.semaphore_signal(barrier, inc=1, device_id=(dp_peer(step), tm), device_id_type=MESH)
+
+    for load in loads[:3]:
+        load.start()
 
     def wait_bytes(like, sem):
         pltpu.make_async_copy(like, like, sem).wait()
@@ -416,7 +417,7 @@
             dst_ref=summed,
             send_sem=send_sem.at[4],
             recv_sem=recv_sem.at[4],
-            device_id=(dp_peer(step), tm),
+            device_id=(dp_peer(dp_size - 2 - step), tm),
             device_id_type=MESH,
         ).start()
 

time: 30.5 us -> 30.8 us (level)
  Pallas kernels: 29 us -> 29.4 us
    pallas_call x1, Pallas kernels: 28.2 us -> 28.6 us  [local(): pl.pallas_call(functools.partial(kernel, tm_size, dp_size), out_shape=[pl...]
where the time goes in v9:
time: 30.8 us; the launch traced here: 30.6 us
  Pallas kernels  29.4 us (95%)
  between operations  1.29 us (4%)
    pallas_call x1, Pallas kernels, local(): pl.pallas_call(functools.partial(kernel, tm_size, dp_size), out_shape=[pl...  28.6 us
    pallas_call x1, Pallas kernels, local(): pl.pallas_call(finish, out_shape=[block, block, block], in_specs=[vmem] *...  0.78 us

profile of v9, /device:TPU:1, one launch (start us, length us, event | category | flops | bytes accessed | tf_op | source)
XLA Modules:
  0.0 30.6 jit_solution(16437829774371936169)
XLA Ops:
  1.3 28.6 %shard_map.103 = (f32[128,256]{1,0:T(8,128)S(1)}, f32[128,256]{1,0:T(8,128)S(1)}, f32[32,8,128]{2,1,0:T(8,128)S(1)}) custom-call(s32[1]{0:T(128)S(6)} %copy.11.ids_hbm, bf16[128,256]{1,0:T(8,128)(2,1)} %bitcast.7, bf16[128,256]{1,0:T(8,128)(2,1)} %bitcast.8, f32[128,256]{1,0:T(8,128)} %filt_hbm.1, f32[3,256]{1,0:T(4,128)} %taps_hbm.1, f32[1,256]{1,0:T(1,128)} %bitcast.9, ...), custom_call_target="tpu_custom_call" | custom-call | tf_op jit(solution)/shard_map/pallas_call | solution.py:472
  29.9 0.8 %shard_map.104 = (f32[128,256]{1,0:T(8,128)}, f32[128,256]{1,0:T(8,128)}, f32[128,256]{1,0:T(8,128)}) custom-call(f32[128,256]{1,0:T(8,128)S(1)} %get-tuple-element.9.layer_in, f32[128,256]{1,0:T(8,128)S(1)} %get-tuple-element.10.gradw_in, f32[32,8,128]{2,1,0:T(8,128)S(1)} %get-tuple-element.11.third), custom_call_target="tpu_custom_call" | custom-call | tf_op jit(solution)/shard_map/pallas_call | solution.py:521

commit v10 on v8

--- a/solution.py
+++ b/solution.py
@@ -381,21 +381,7 @@
     layer = to_blocks(convolved) + gain * value
     middle = (to_blocks(correlated) + gain * grad) * scale
     encode_two(layer, stencil(middle, taps[::-1]), send_c)
-    @pl.loop(0, tm_size)
-    def _(step):
-        peer = lax.rem(place + far_first(lax.rem(step, per), per), per) * dp_size + lax.div(step, per)
-
-        @pl.when(peer != tm)
-        def _():
-            pltpu.make_async_remote_copy(
-                src_ref=send_c.at[peer],
-                dst_ref=recv_c.at[tm],
-                send_sem=send_sem.at[3],
-                recv_sem=recv_sem.at[3],
-                device_id=(dp, peer),
-                device_id_type=MESH,
-            ).start()
-
+    exchange(send_c, recv_c, 3)
     recv_c[tm] = send_c[tm]
 
     @pl.when(adder == dp)

time: 30.5 us -> 30.7 us (level)
  no operation moved by 1% of the time
where the time goes in v10:
time: 30.7 us; the launch traced here: 30.6 us
  Pallas kernels  29.3 us (95%)
  between operations  1.29 us (4%)
    pallas_call x1, Pallas kernels, local(): pl.pallas_call(functools.partial(kernel, tm_size, dp_size), out_shape=[pl...  28.5 us
    pallas_call x1, Pallas kernels, local(): pl.pallas_call(finish, out_shape=[block, block, block], in_specs=[vmem] *...  0.78 us

profile of v10, /device:TPU:1, one launch (start us, length us, event | category | flops | bytes accessed | tf_op | source)
XLA Modules:
  0.0 30.6 jit_solution(1904046970234039624)
XLA Ops:
  1.3 28.5 %shard_map.103 = (f32[128,256]{1,0:T(8,128)S(1)}, f32[128,256]{1,0:T(8,128)S(1)}, f32[32,8,128]{2,1,0:T(8,128)S(1)}) custom-call(s32[1]{0:T(128)S(6)} %copy.11.ids_hbm, bf16[128,256]{1,0:T(8,128)(2,1)} %bitcast.7, bf16[128,256]{1,0:T(8,128)(2,1)} %bitcast.8, f32[128,256]{1,0:T(8,128)} %filt_hbm.1, f32[3,256]{1,0:T(4,128)} %taps_hbm.1, f32[1,256]{1,0:T(1,128)} %bitcast.9, ...), custom_call_target="tpu_custom_call" | custom-call | tf_op jit(solution)/shard_map/pallas_call | solution.py:457
  29.8 0.8 %shard_map.104 = (f32[128,256]{1,0:T(8,128)}, f32[128,256]{1,0:T(8,128)}, f32[128,256]{1,0:T(8,128)}) custom-call(f32[128,256]{1,0:T(8,128)S(1)} %get-tuple-element.9.layer_in, f32[128,256]{1,0:T(8,128)S(1)} %get-tuple-element.10.gradw_in, f32[32,8,128]{2,1,0:T(8,128)S(1)} %get-tuple-element.11.third), custom_call_target="tpu_custom_call" | custom-call | tf_op jit(solution)/shard_map/pallas_call | solution.py:506
